TPU v7x, 32 devices: a whole 2x2x4 slice. The times are simulated.
32 devices in a mesh: seg: 8 (over z, y), grp: 4 (over x, core).
Axes of the slice: x: 2, y: 2, z: 4, core: 2. Of those that a mesh axis runs over, the one named last changes fastest.
Arguments:
- spectra: bfloat16 [8, 2, 128, 12288], P(None, None, None, ('seg', 'grp'))
- band_bins: int32 [2, 2], replicated, may hold values from 0 to 80, as said below
- far_list: int32 [4, 8, 8, 4, 3], P('grp'), may hold values from 0 to 2, as said below
- far_count: int32 [4, 8, 8], P('grp'), may hold values from 0 to 4, as said below
Outputs:
- near_corr: bfloat16 [2, 2, 12288, 1536], P(None, None, ('seg', 'grp'))
- far_corr: bfloat16 [8, 4, 8, 4, 2, 128, 128], P('seg', 'grp')
Inputs may be any that keep to these rules, and one draw needn't show every extreme that they name: band_bins[b, 0] + 48 <= 128 and 1 <= band_bins[b, 1] <= 48; band 0 has exactly 48 bins; one band starts at bin 0 and the other at bin 128 - 48. far_list entries: row and column blocks 0 to 2, band 0 or 1. far_count is 0 where owner and source group are the same; every owner has some source group with exactly 4.
All inputs are finite; a program needn't handle non-finite values.
Results may differ from a plain program's by a relative error of at most 0.0058.
Values may be sent and summed in bfloat16 or wider, within the bound.
A program may use at most 192 MiB of HBM per device.

v0:
```python
import functools

import jax
import jax.numpy as jnp
from jax import lax
from jax.experimental import pallas as pl
from jax.experimental.pallas import tpu as pltpu
from jax.sharding import PartitionSpec as P

W = 8
F = 128
BAND_MAX = 48
SMOOTH = 4
BLOCK = 128
BLK_DEV = 3
DEPTH = W * 2 * BAND_MAX
PIECES = 2 * BLK_DEV
LINE_Z = 4
CORES = 2


HIGH = lax.Precision.HIGHEST
MESH = pl.DeviceIdType.MESH


def whiten_kernel(bins, spectra, cols, gain):
    power = jnp.zeros((F, BLOCK), jnp.float32)
    for w in range(W):
        for p in range(2):
            values = spectra[w, p].astype(jnp.float32)
            power = power + values * values
    f = lax.broadcasted_iota(jnp.int32, (F, F), 0)
    g = lax.broadcasted_iota(jnp.int32, (F, F), 1)
    window = jnp.where(jnp.abs(f - g) <= SMOOTH, 1.0, 0.0).astype(jnp.float32)
    totals = jnp.sum(window, axis=1, keepdims=True) * W
    level = jnp.dot(window, power, precision=HIGH, preferred_element_type=jnp.float32) / totals
    gain[...] = lax.rsqrt(level + 1e-06)
    for band in range(2):
        at = pl.ds(pl.multiple_of(bins[band, 0], 16), BAND_MAX)
        scale = gain[at]
        for p in range(2):
            for w in range(W):
                first = (p * W + w) * BAND_MAX
                piece = spectra[w, p, at].astype(jnp.float32) * scale
                cols[band, 0, first : first + BAND_MAX] = piece.astype(jnp.bfloat16)


def band_columns(spectra, band_bins):
    return pl.pallas_call(
        whiten_kernel,
        grid=(BLK_DEV,),
        out_shape=jax.ShapeDtypeStruct((2, BLK_DEV, DEPTH, BLOCK), jnp.bfloat16),
        in_specs=[
            pl.BlockSpec(memory_space=pltpu.SMEM),
            pl.BlockSpec((W, 2, F, BLOCK), lambda m: (0, 0, 0, m)),
        ],
        out_specs=pl.BlockSpec((2, 1, DEPTH, BLOCK), lambda m: (0, m, 0, 0)),
        scratch_shapes=[pltpu.VMEM((F, BLOCK), jnp.float32)],
        compiler_params=pltpu.CompilerParams(vmem_limit_bytes=56 * 1024 * 1024),
    )(band_bins, spectra).reshape(PIECES, DEPTH, BLOCK)


class Gather:
    def __init__(self, axis, high, low, own, buf, send, recv):
        self.axis, self.high, self.low = axis, high, low
        self.own, self.buf, self.send, self.recv = own, buf, send, recv
        self.me = lax.axis_index(axis)
        self.p, self.l = lax.div(self.me, low), lax.rem(self.me, low)
        p, l = self.p, self.l
        self.dirs = [
            (p + 1 < high, self.me + low),
            (p > 0, self.me - low),
            (l + 1 < low, self.me + 1),
            (l > 0, self.me - 1),
        ]
        if high == 1:
            self.dirs[0] = self.dirs[1] = None
        if low == 1:
            self.dirs[2] = self.dirs[3] = None
        self.closing = False

    def greet(self, barrier):
        for entry in self.dirs:
            if entry is not None:

                @pl.when(entry[0])
                def _():
                    pl.semaphore_signal(
                        barrier, inc=1, device_id={self.axis: entry[1]}, device_id_type=MESH
                    )

    def peers(self):
        return sum(jnp.where(entry[0], 1, 0) for entry in self.dirs if entry is not None)

    def copy(self, way, src, q, own):
        return pltpu.make_async_remote_copy(
            src_ref=self.own.at[q] if own else self.buf.at[src, q],
            dst_ref=self.buf.at[src, q],
            send_sem=self.send.at[way, src, q],
            recv_sem=self.recv.at[src, q],
            device_id={self.axis: self.dirs[way][1]},
            device_id_type=MESH,
        )

    def pass_on(self, ways, src, q, own=False):
        for way in ways:
            if self.dirs[way] is not None:

                @pl.when(self.dirs[way][0])
                def _():
                    piece = self.copy(way, src, q, own)
                    if self.closing:
                        piece.wait_send()
                    else:
                        piece.start()

    def arrive(self, there, src, q, ways, use):
        @pl.when(there)
        def _():
            if not self.closing:
                pltpu.make_async_copy(
                    self.buf.at[src, q], self.buf.at[src, q], self.recv.at[src, q]
                ).wait()
            self.pass_on(ways, src, q)
            if use is not None and not self.closing:
                use(src, q)

    def start(self, q):
        self.pass_on((0, 1, 2, 3), self.me, q, own=True)

    def step(self, st, q, use, low_first=False):
        p, l, low = self.p, self.l, self.low
        turn = () if low_first else (2, 3)
        if 0 < st < self.high:
            self.arrive(p - st >= 0, (p - st) * low + l, q, (0,) + turn, use)
            self.arrive(p + st < self.high, (p + st) * low + l, q, (1,) + turn, use)
        d = st - 1
        if not 0 <= d < self.high:
            return
        for far, way in [(p, None)] if d == 0 else [(p - d, 0), (p + d, 1)]:
            inside = (far >= 0) & (far < self.high)
            for e in range(1, low):
                for there, other, on in ((l - e >= 0, l - e, 2), (l + e < low, l + e, 3)):
                    if not low_first:
                        ways = (on,)
                    elif d == 0:
                        ways = (0, 1, on)
                    else:
                        ways = (way,)
                    self.arrive(inside & there, far * low + other, q, ways, use)


def kernel(
    nseg, ngrp, bins, lists, counts, cols, near, far, seg_buf, grp_buf, ops,
    seg_send, seg_recv, grp_send, grp_recv, move,
):
    seg = Gather("seg", LINE_Z, nseg // LINE_Z, cols, seg_buf, seg_send, seg_recv)
    grp = Gather("grp", ngrp // CORES, CORES, cols, grp_buf, grp_send, grp_recv)
    barrier = pltpu.get_barrier_semaphore()
    seg.greet(barrier)
    grp.greet(barrier)
    pl.semaphore_wait(barrier, seg.peers() + grp.peers())

    def loop(fn, first=0):
        def step(q, carry):
            fn(q)
            return carry

        lax.fori_loop(first, PIECES, step, 0)

    def begin(q):
        seg.start(q)
        grp.start(q)

    loop(begin)
    own = pltpu.make_async_copy(cols, seg_buf.at[seg.me], move)
    own.start()

    half = DEPTH // 2

    def operands(q):
        band, m = lax.div(q, BLK_DEV), lax.rem(q, BLK_DEV)
        bin_of = lax.rem(lax.broadcasted_iota(jnp.int32, (1, DEPTH), 1), BAND_MAX)
        live = jnp.where(bin_of < bins[band, 1], 1.0, 0.0).astype(jnp.float32)
        rows = jnp.transpose(cols[q].astype(jnp.float32)) * live
        ops[band, m, :BLOCK] = rows.astype(jnp.bfloat16)
        ops[band, m, BLOCK:, :half] = rows[:, half:].astype(jnp.bfloat16)
        ops[band, m, BLOCK:, half:] = (-rows[:, :half]).astype(jnp.bfloat16)

    loop(operands)

    def scale(band):
        return lax.rsqrt(jnp.full((1, BLOCK), W * bins[band, 1], jnp.int32).astype(jnp.float32))

    def near_from(piece, src, q):
        band, m = lax.div(q, BLK_DEV), lax.rem(q, BLK_DEV)
        at = pl.ds(pl.multiple_of(src * (BLK_DEV * BLOCK) + m * BLOCK, BLOCK), BLOCK)
        for i in range(BLK_DEV):
            prod = jnp.dot(ops[band, i], piece, preferred_element_type=jnp.float32)
            prod = (prod * scale(band)).astype(jnp.bfloat16)
            near[band, 0, i * BLOCK : (i + 1) * BLOCK, at] = prod[:BLOCK]
            near[band, 1, i * BLOCK : (i + 1) * BLOCK, at] = prod[BLOCK:]

    def use_near(src, q):
        near_from(grp_buf[src, q], src, q)

    loop(lambda q: near_from(cols[q], grp.me, q))

    def steps():
        for st in range(1, max(seg.high, grp.high) + 1):

            def both(q, low_first=False):
                seg.step(st, q, None, low_first)
                grp.step(st, q, use_near)

            both(jnp.int32(0), low_first=True)
            loop(both, 1)

    steps()
    own.wait()

    slots = far.shape[1]

    def far_source(t, carry):
        for c in range(slots):
            entry = (t * slots + c) * 3
            i = lists[seg.me, entry]
            m = lists[seg.me, entry + 1]
            band = lists[seg.me, entry + 2]
            factor = jnp.where(c < counts[seg.me, t], scale(band), 0.0)
            prod = jnp.dot(
                ops[band, i], seg_buf[t, band * BLK_DEV + m], preferred_element_type=jnp.float32
            )
            prod = (prod * factor).astype(jnp.bfloat16)
            far[t, c, 0] = prod[:BLOCK]
            far[t, c, 1] = prod[BLOCK:]
        return carry

    lax.fori_loop(0, nseg, far_source, 0)

    seg.closing = grp.closing = True
    loop(begin)
    steps()


def body(nseg, ngrp, spectra, band_bins, far_list, far_count):
    cols = band_columns(spectra, band_bins)
    slots = far_list.shape[3]
    smem = pl.BlockSpec(memory_space=pltpu.SMEM)
    whole = pl.BlockSpec(memory_space=pltpu.VMEM)
    sems = pltpu.SemaphoreType.DMA
    shard = PIECES * DEPTH * BLOCK * 2
    result = (2 * 2 * BLK_DEV * BLOCK * ngrp * BLK_DEV + nseg * slots * 2 * BLOCK) * BLOCK * 2
    vmem = (nseg + ngrp + 4) * shard + result + 2 * 1024 * 1024
    near, far = pl.pallas_call(
        functools.partial(kernel, nseg, ngrp),
        out_shape=(
            jax.ShapeDtypeStruct(
                (2, 2, BLK_DEV * BLOCK, ngrp * BLK_DEV * BLOCK), jnp.bfloat16
            ),
            jax.ShapeDtypeStruct((nseg, slots, 2, BLOCK, BLOCK), jnp.bfloat16),
        ),
        in_specs=[smem, smem, smem, whole],
        out_specs=(whole, whole),
        scratch_shapes=[
            pltpu.VMEM((nseg, PIECES, DEPTH, BLOCK), jnp.bfloat16),
            pltpu.VMEM((ngrp, PIECES, DEPTH, BLOCK), jnp.bfloat16),
            pltpu.VMEM((2, BLK_DEV, 2 * BLOCK, DEPTH), jnp.bfloat16),
            sems((4, nseg, PIECES)),
            sems((nseg, PIECES)),
            sems((4, ngrp, PIECES)),
            sems((ngrp, PIECES)),
            sems,
        ],
        compiler_params=pltpu.CompilerParams(
            collective_id=0, has_side_effects=True, vmem_limit_bytes=vmem
        ),
    )(band_bins, far_list.reshape(nseg, nseg * slots * 3), far_count[0], cols)
    return (near, far[None, None])


def solution(mesh):
    placed = (
        P(None, None, None, ("seg", "grp")),
        P(),
        P("grp", None, None, None, None),
        P("grp", None, None),
    )
    return jax.shard_map(
        functools.partial(body, mesh.shape["seg"], mesh.shape["grp"]),
        mesh=mesh,
        in_specs=placed,
        out_specs=(
            P(None, None, ("seg", "grp"), None),
            P("seg", "grp", None, None, None, None, None),
        ),
        check_vma=False,
    )
```

profile of v0, /device:TPU:0, one launch (start us, length us, event | category | flops | bytes accessed | tf_op | source)
XLA Modules:
  0.0 115.5 jit_solution(16777050428398514093)
XLA Ops:
  0.6 0.0 copy-start.1
  0.6 0.0 copy-start.2
  0.7 0.9 copy.7
  1.6 0.1 copy.8.lists
  1.7 3.7 %shard_map.59 = bf16[2,3,768,128]{3,2,1,0:T(8,128)(2,1)} custom-call(s32[2,2]{1,0:T(2,128)} %bins.3, bf16[8,2,128,384]{3,2,1,0:T(8,128)(2,1)} %spectra.1), custom_call_target="tpu_custom_call" | custom-call | tf_op jit(solution)/shard_map/pallas_call | solution.py:49
  5.4 0.0 copy-done.1
  5.4 0.0 copy-done.2
  5.4 0.0 copy-start
  5.4 1.3 %copy-done = bf16[2,3,768,128]{3,2,1,0:T(8,128)(2,1)S(1)} copy-done((bf16[2,3,768,128]{3,2,1,0:T(8,128)(2,1)S(1)}, bf16[2,3,768,128]{3,2,1,0:T(8,128)(2,1)}, u32[]{:S(2)}) %copy-start) | copy-done | bytes 1179672
  6.6 105.4 %shard_map.60 = (bf16[2,2,384,1536]{3,2,1,0:T(8,128)(2,1)S(1)}, bf16[8,4,2,128,128]{4,3,2,1,0:T(8,128)(2,1)S(1)}) custom-call(s32[2,2]{1,0:T(2,128)S(1)} %copy-done.1, s32[8,96]{1,0:T(8,128)S(1)} %copy.8.lists, s32[8,8]{1,0:T(8,128)S(1)} %bitcast.7, bf16[6,768,128]{2,1,0:T(8,128)(2,1)S(1)} %bitcast.5), custom_call_target="tpu_custom_call" | custom-call | tf_op jit(solution)/shard_map/pallas_call | solution.py:255
  112.0 2.2 %copy.11 = bf16[2,2,384,1536]{3,2,1,0:T(8,128)(2,1)} copy(bf16[2,2,384,1536]{3,2,1,0:T(8,128)(2,1)S(1)} %get-tuple-element.8) | data formatting | bytes 9437184
  114.2 1.3 %copy.12 = bf16[1,1,8,4,2,128,128]{6,5,4,3,2,1,0:T(8,128)(2,1)} copy(bf16[1,1,8,4,2,128,128]{6,5,4,3,2,1,0:T(8,128)(2,1)S(1)} %bitcast.6) | data formatting | bytes 4194304
  (1 shorter events, 0.0 us)
Async XLA Ops:
  0.6 4.7 %copy-start.1 = (s32[2,2]{1,0:T(2,128)S(1)}, s32[2,2]{1,0:T(2,128)}, u32[]{:S(2)}) copy-start(s32[2,2]{1,0:T(2,128)} %bins.3) | copy-start | bytes 52
  0.6 4.7 %copy-start.2 = (s32[1,8,8]{2,1,0:T(8,128)S(1)}, s32[1,8,8]{2,1,0:T(8,128)}, u32[]{:S(2)}) copy-start(s32[1,8,8]{2,1,0:T(8,128)} %param.7) | copy-start | bytes 772
  5.4 1.3 %copy-start = (bf16[2,3,768,128]{3,2,1,0:T(8,128)(2,1)S(1)}, bf16[2,3,768,128]{3,2,1,0:T(8,128)(2,1)}, u32[]{:S(2)}) copy-start(bf16[2,3,768,128]{3,2,1,0:T(8,128)(2,1)} %shard_map.59) | copy-start | bytes 3538948
where the time goes:
time: 116 us
  Pallas kernels  109 us (94%)
  local copies, waits for them, and re-layouts  5.77 us (5%)
    pallas_call x1, Pallas kernels, body(): pl.pallas_call(functools.partial(kernel, nseg, ngrp), out_shape=(jax.Shap...  105 us
    unnamed x9, local copies, waits for them, and re-layouts  5.69 us
    pallas_call x1, Pallas kernels, band_columns(): pl.pallas_call(whiten_kernel, grid=(BLK_DEV,), out_shape=jax.ShapeDtypeSt...  3.71 us

commit v1 on v0

v1 whole, which is shorter than its diff:
```python
import functools
import math

import jax
import jax.numpy as jnp
from jax import lax
from jax.experimental import pallas as pl
from jax.experimental.pallas import tpu as pltpu
from jax.sharding import PartitionSpec as P

W = 8
F = 128
BAND_MAX = 48
SMOOTH = 4
BLOCK = 128
BLK_DEV = 3
DEPTH = W * 2 * BAND_MAX
PIECES = 2 * BLK_DEV
LEVELS = 4
CORES = 2


HIGH = lax.Precision.HIGHEST
MESH = pl.DeviceIdType.MESH


def whiten(m, bins, spec, cols):
    power = jnp.zeros((F, BLOCK), jnp.float32)
    for w in range(W):
        for p in range(2):
            values = spec[m % 2, w, p].astype(jnp.float32)
            power = power + values * values
    f = lax.broadcasted_iota(jnp.int32, (F, F), 0)
    g = lax.broadcasted_iota(jnp.int32, (F, F), 1)
    window = jnp.where(jnp.abs(f - g) <= SMOOTH, 1.0, 0.0).astype(jnp.float32)
    totals = jnp.sum(window, axis=1, keepdims=True) * W
    level = jnp.dot(window, power, precision=HIGH, preferred_element_type=jnp.float32) / totals
    gain = lax.rsqrt(level + 1e-06)
    ahead = jnp.full((BAND_MAX, BLOCK), bins[0, 0], jnp.int32) == 0
    for p in range(2):
        for w in range(W):
            at = slice((p * W + w) * BAND_MAX, (p * W + w + 1) * BAND_MAX)
            low = spec[m % 2, w, p, :BAND_MAX].astype(jnp.float32) * gain[:BAND_MAX]
            high = spec[m % 2, w, p, F - BAND_MAX :].astype(jnp.float32) * gain[F - BAND_MAX :]
            cols[m * 2, at] = jnp.where(ahead, low, high).astype(jnp.bfloat16)
            cols[m * 2 + 1, at] = jnp.where(ahead, high, low).astype(jnp.bfloat16)


class Gather:
    def __init__(self, axis, high, low, own, buf, send, recv):
        self.axis, self.high, self.low = axis, high, low
        self.own, self.buf, self.send, self.recv = own, buf, send, recv
        self.me = lax.axis_index(axis)
        self.p, self.l = lax.div(self.me, low), lax.rem(self.me, low)
        p, l = self.p, self.l
        self.dirs = [
            (p + 1 < high, self.me + low),
            (p > 0, self.me - low),
            (l + 1 < low, self.me + 1),
            (l > 0, self.me - 1),
        ]
        if high == 1:
            self.dirs[0] = self.dirs[1] = None
        if low == 1:
            self.dirs[2] = self.dirs[3] = None
        self.closing = False

    def greet(self, barrier):
        for entry in self.dirs:
            if entry is not None:

                @pl.when(entry[0])
                def _():
                    pl.semaphore_signal(
                        barrier, inc=1, device_id={self.axis: entry[1]}, device_id_type=MESH
                    )

    def peers(self):
        return sum(jnp.where(entry[0], 1, 0) for entry in self.dirs if entry is not None)

    def copy(self, way, src, q, own):
        return pltpu.make_async_remote_copy(
            src_ref=self.own.at[q] if own else self.buf.at[src, q],
            dst_ref=self.buf.at[src, q],
            send_sem=self.send.at[way, src, q],
            recv_sem=self.recv.at[src, q],
            device_id={self.axis: self.dirs[way][1]},
            device_id_type=MESH,
        )

    def pass_on(self, ways, src, q, own=False):
        for way in ways:
            if self.dirs[way] is not None:

                @pl.when(self.dirs[way][0])
                def _():
                    piece = self.copy(way, src, q, own)
                    if self.closing:
                        piece.wait_send()
                    else:
                        piece.start()

    def arrive(self, there, src, q, ways, use):
        @pl.when(there)
        def _():
            if not self.closing:
                pltpu.make_async_copy(
                    self.buf.at[src, q], self.buf.at[src, q], self.recv.at[src, q]
                ).wait()
            self.pass_on(ways, src, q)
            if use is not None and not self.closing:
                use(src, q)

    def start(self, q):
        self.pass_on((0, 1, 2, 3), self.me, q, own=True)

    def step(self, st, q, use, low_first=False):
        p, l, low = self.p, self.l, self.low
        turn = () if low_first else (2, 3)
        if 0 < st < self.high:
            self.arrive(p - st >= 0, (p - st) * low + l, q, (0,) + turn, use)
            self.arrive(p + st < self.high, (p + st) * low + l, q, (1,) + turn, use)
        d = st - 1
        if not 0 <= d < self.high:
            return
        for far, way in [(p, None)] if d == 0 else [(p - d, 0), (p + d, 1)]:
            inside = (far >= 0) & (far < self.high)
            for e in range(1, low):
                for there, other, on in ((l - e >= 0, l - e, 2), (l + e < low, l + e, 3)):
                    if not low_first:
                        ways = (on,)
                    elif d == 0:
                        ways = (0, 1, on)
                    else:
                        ways = (way,)
                    self.arrive(inside & there, far * low + other, q, ways, use)


class Line:
    def __init__(self, low, own, bufs, send, recv):
        self.low, self.own, self.bufs, self.send, self.recv = low, own, bufs, send, recv
        self.me = lax.axis_index("seg")
        self.z = lax.div(self.me, low)
        self.closing = False

    def slot(self, d, way):
        return d if d > 1 else 1 - way

    def buf(self, d, way):
        return self.bufs[self.slot(d, way)]

    def move(self, way, d, q):
        at = self.slot(d + 1, way)
        piece = pltpu.make_async_remote_copy(
            src_ref=self.buf(d, way).at[q] if d else self.own.at[q],
            dst_ref=self.bufs[at].at[q],
            send_sem=self.send.at[way, d, q],
            recv_sem=self.recv.at[at, q],
            device_id={"seg": self.me + (self.low if way else -self.low)},
            device_id_type=MESH,
        )
        if self.closing:
            piece.wait_send()
        else:
            piece.start()

    def start(self, q):
        z = self.z

        @pl.when((z + 1 < LEVELS) & (z != LEVELS - 2))
        def _():
            self.move(1, 0, q)

        @pl.when((z > 0) & (z != 1))
        def _():
            self.move(0, 0, q)

    def there(self, d):
        z = self.z
        left, right = z - d >= 0, z + d < LEVELS
        if d == 1:
            left, right = left & (z != LEVELS - 1), right & (z != 0)
        return ((left, z - d, z + 1 < LEVELS, 1), (right, z + d, z > 0, 0))

    def arrive(self, d, q):
        for here, _, on, way in self.there(d):

            @pl.when(here)
            def _():
                if not self.closing:
                    at = self.slot(d, way)
                    piece = self.bufs[at].at[q]
                    pltpu.make_async_copy(piece, piece, self.recv.at[at, q]).wait()

                if d + 1 < LEVELS:

                    @pl.when(on)
                    def _():
                        self.move(way, d, q)


def kernel(
    nseg, ngrp, bins, lists, counts, spectra, near, far,
    spec, cols, left, right, two, three, side, grp_buf, ops, stage, end_stage,
    spec_sem, line_send, line_recv, side_send, side_recv, grp_send, grp_recv,
    far_send, end_send, far_recv, move,
):
    low = nseg // LEVELS
    slots = far.shape[1]
    line = Line(low, cols, (left, right, two, three), line_send, line_recv)
    grp = Gather("grp", ngrp // CORES, CORES, cols, grp_buf, grp_send, grp_recv)
    me, z = line.me, line.z
    y = lax.rem(me, low)
    mates = [lax.rem(y + e, low) for e in range(1, low)]
    is_end = (z == 0) | (z == LEVELS - 1)
    inner = (z == 1) | (z == LEVELS - 2)
    end = jnp.where(z == 1, 0, LEVELS - 1)
    beside = jnp.where(z == 0, 1, LEVELS - 2)

    def load(m):
        return pltpu.make_async_copy(
            spectra.at[:, :, :, m * BLOCK : (m + 1) * BLOCK], spec.at[m % 2], spec_sem.at[m % 2]
        )

    load(0).start()
    load(1).start()

    barrier = pltpu.get_barrier_semaphore()

    def greet(seg):
        pl.semaphore_signal(barrier, inc=1, device_id={"seg": seg}, device_id_type=MESH)

    for on, seg in ((z + 1 < LEVELS, me + low), (z > 0, me - low)):

        @pl.when(on)
        def _():
            greet(seg)

    for mate in mates:
        greet(z * low + mate)
    grp.greet(barrier)

    def side_copy(e, q):
        return pltpu.make_async_remote_copy(
            src_ref=cols.at[q],
            dst_ref=side.at[y, q],
            send_sem=side_send.at[e, q],
            recv_sem=side_recv.at[y, q],
            device_id={"seg": z * low + mates[e]},
            device_id_type=MESH,
        )

    def begin(q):
        line.start(q)
        for e in range(low - 1):
            if line.closing:
                side_copy(e, q).wait_send()
            else:
                side_copy(e, q).start()
        grp.start(q)

    def loop(fn, count=PIECES):
        def step(q, carry):
            fn(q)
            return carry

        lax.fori_loop(0, count, step, 0)

    for m in range(BLK_DEV):
        load(m).wait()
        whiten(m, bins, spec, cols)
        if m + 2 < BLK_DEV:
            load(m + 2).start()
        if m == 0:
            inner_peers = jnp.where(z + 1 < LEVELS, 1, 0) + jnp.where(z > 0, 1, 0)
            pl.semaphore_wait(barrier, inner_peers + (low - 1) + grp.peers())
        begin(2 * m)
        begin(2 * m + 1)

    own = pltpu.make_async_copy(cols, side.at[y], move)
    own.start()

    half = DEPTH // 2

    def operands(slot, q, piece):
        band = lax.rem(q, 2)
        bin_of = lax.rem(lax.broadcasted_iota(jnp.int32, (1, DEPTH), 1), BAND_MAX)
        live = jnp.where(bin_of < bins[band, 1], 1.0, 0.0).astype(jnp.float32)
        rows = jnp.transpose(piece.astype(jnp.float32)) * live
        ops[slot, q, :BLOCK] = rows.astype(jnp.bfloat16)
        ops[slot, q, BLOCK:, :half] = rows[:, half:].astype(jnp.bfloat16)
        ops[slot, q, BLOCK:, half:] = (-rows[:, :half]).astype(jnp.bfloat16)

    loop(lambda q: operands(y, q, cols[q]))

    def scale(band):
        return lax.rsqrt(jnp.full((1, BLOCK), W * bins[band, 1], jnp.int32).astype(jnp.float32))

    def near_from(piece, src, q):
        m, band = lax.div(q, 2), lax.rem(q, 2)
        at = pl.ds(pl.multiple_of(src * (BLK_DEV * BLOCK) + m * BLOCK, BLOCK), BLOCK)
        for i in range(BLK_DEV):
            prod = jnp.dot(ops[y, i * 2 + band], piece, preferred_element_type=jnp.float32)
            prod = (prod * scale(band)).astype(jnp.bfloat16)
            near[band, 0, i * BLOCK : (i + 1) * BLOCK, at] = prod[:BLOCK]
            near[band, 1, i * BLOCK : (i + 1) * BLOCK, at] = prod[BLOCK:]

    def use_near(src, q):
        near_from(grp_buf[src, q], src, q)

    loop(lambda q: near_from(cols[q], grp.me, q))

    def pair(owner, slot, src, t, dst, c):
        i, m, band = lists[owner, 0, c, t], lists[owner, 1, c, t], lists[owner, 2, c, t]
        factor = jnp.where(c < counts[owner, t], scale(band), 0.0)
        prod = jnp.dot(
            ops[slot, i * 2 + band], src[m * 2 + band], preferred_element_type=jnp.float32
        )
        prod = (prod * factor).astype(jnp.bfloat16)
        dst[c, 0] = prod[:BLOCK]
        dst[c, 1] = prod[BLOCK:]

    def level_pairs(buf, src, c):
        t = src * low + y
        pair(me, y, buf, t, far.at[t], c)
        for mate in mates:
            pair(z * low + mate, mate, buf, t, stage.at[mate, src], c)

    def hand_over(src):
        for mate in mates:
            piece = pltpu.make_async_remote_copy(
                src_ref=stage.at[mate, src],
                dst_ref=far.at[src * low + y],
                send_sem=far_send.at[mate, src],
                recv_sem=far_recv.at[src * low + y],
                device_id={"seg": z * low + mate},
                device_id_type=MESH,
            )
            if line.closing:
                piece.wait_send()
            else:
                piece.start()

    def end_copy(other):
        return pltpu.make_async_remote_copy(
            src_ref=end_stage.at[other],
            dst_ref=far.at[z * low + other],
            send_sem=end_send.at[other],
            recv_sem=far_recv.at[z * low + other],
            device_id={"seg": end * low + y},
            device_id_type=MESH,
        )

    def for_end():
        for at, buf in ((1, left), (LEVELS - 2, right)):

            @pl.when(z == at)
            def _():
                loop(lambda q: operands(low, q, buf[q]))

        @pl.when(inner)
        def _():
            for other in [y] + mates:
                t = z * low + other
                loop(
                    lambda c: pair(end * low + y, low, side.at[other], t, end_stage.at[other], c),
                    slots,
                )
                end_copy(other).start()

    def first(q):
        line.arrive(1, q)
        grp.step(1, q, None if grp.closing else use_near)
        if not line.closing:
            for mate in mates:
                pltpu.make_async_copy(
                    side.at[mate, q], side.at[mate, q], side_recv.at[mate, q]
                ).wait()
                operands(mate, q, side[mate, q])

    def second(q):
        line.arrive(2, q)
        grp.step(2, q, None if grp.closing else use_near)
        if not line.closing:

            @pl.when(q < slots)
            def _():
                for mate in mates:
                    t = z * low + mate
                    pair(me, y, side.at[mate], t, far.at[t], q)
                for here, src, _, way in line.there(1):

                    @pl.when(here)
                    def _():
                        level_pairs(line.buf(1, way), src, q)

                        @pl.when(q == slots - 1)
                        def _():
                            hand_over(src)

    def later(d):
        def step(q):
            if d < LEVELS:
                line.arrive(d, q)
            grp.step(d, q, None if grp.closing else use_near)

        loop(step)

    def after(d):
        for here, src, _, way in line.there(d):

            @pl.when(here)
            def _():
                if not line.closing:
                    loop(lambda c: level_pairs(line.buf(d, way), src, c), slots)
                hand_over(src)

    loop(first)
    own.wait()
    far[me] = jnp.zeros(far.shape[1:], far.dtype)
    for_end()
    loop(second)
    after(2)
    for d in range(3, max(LEVELS, grp.high + 1)):
        later(d)
        if d < LEVELS:
            after(d)

    line.closing = grp.closing = True
    loop(begin)
    loop(first)
    after(1)
    loop(second)
    after(2)
    for d in range(3, max(LEVELS, grp.high + 1)):
        later(d)
        if d < LEVELS:
            after(d)

    @pl.when(inner)
    def _():
        for other in [y] + mates:
            end_copy(other).wait_send()

    def landed(t):
        tz, ty = lax.div(t, low), lax.rem(t, low)

        @pl.when(((ty != y) & (tz != z)) | (is_end & (tz == beside) & (ty == y)))
        def _():
            pltpu.make_async_copy(far.at[t], far.at[t], far_recv.at[t]).wait()

    loop(landed, nseg)


def body(nseg, ngrp, spectra, band_bins, far_list, far_count):
    slots = far_list.shape[3]
    low = nseg // LEVELS
    smem = pl.BlockSpec(memory_space=pltpu.SMEM)
    whole = pl.BlockSpec(memory_space=pltpu.VMEM)
    sems = pltpu.SemaphoreType.DMA
    half = jnp.bfloat16
    near = jax.ShapeDtypeStruct((2, 2, BLK_DEV * BLOCK, ngrp * BLK_DEV * BLOCK), half)
    far = jax.ShapeDtypeStruct((nseg, slots, 2, BLOCK, BLOCK), half)
    buffers = [
        pltpu.VMEM((2, W, 2, F, BLOCK), half),
        pltpu.VMEM((PIECES, DEPTH, BLOCK), half),
        pltpu.VMEM((PIECES, DEPTH, BLOCK), half),
        pltpu.VMEM((PIECES, DEPTH, BLOCK), half),
        pltpu.VMEM((PIECES, DEPTH, BLOCK), half),
        pltpu.VMEM((PIECES, DEPTH, BLOCK), half),
        pltpu.VMEM((low, PIECES, DEPTH, BLOCK), half),
        pltpu.VMEM((ngrp, PIECES, DEPTH, BLOCK), half),
        pltpu.VMEM((low + 1, PIECES, 2 * BLOCK, DEPTH), half),
        pltpu.VMEM((low, LEVELS, slots, 2, BLOCK, BLOCK), half),
        pltpu.VMEM((low, slots, 2, BLOCK, BLOCK), half),
    ]
    vmem = sum(math.prod(a.shape) * 2 for a in buffers + [near, far]) + 2 * 1024 * 1024
    near, far = pl.pallas_call(
        functools.partial(kernel, nseg, ngrp),
        out_shape=(near, far),
        in_specs=[smem, smem, smem, pl.BlockSpec(memory_space=pl.ANY)],
        out_specs=(whole, whole),
        scratch_shapes=buffers
        + [
            sems((2,)),
            sems((2, LEVELS, PIECES)),
            sems((LEVELS, PIECES)),
            sems((low, PIECES)),
            sems((low, PIECES)),
            sems((4, ngrp, PIECES)),
            sems((ngrp, PIECES)),
            sems((low, LEVELS)),
            sems((low,)),
            sems((nseg,)),
            sems,
        ],
        compiler_params=pltpu.CompilerParams(
            collective_id=0, has_side_effects=True, vmem_limit_bytes=vmem
        ),
    )(band_bins, jnp.transpose(far_list[0], (0, 3, 2, 1)), far_count[0], spectra)
    return (near, far[None, None])


def solution(mesh):
    placed = (
        P(None, None, None, ("seg", "grp")),
        P(),
        P("grp", None, None, None, None),
        P("grp", None, None),
    )
    return jax.shard_map(
        functools.partial(body, mesh.shape["seg"], mesh.shape["grp"]),
        mesh=mesh,
        in_specs=placed,
        out_specs=(
            P(None, None, ("seg", "grp"), None),
            P("seg", "grp", None, None, None, None, None),
        ),
        check_vma=False,
    )
```

time: 116 us -> 92.4 us (0.80)
  Pallas kernels: 109 us -> 84.5 us
  local copies, waits for them, and re-layouts: 5.77 us -> 7.07 us
    pallas_call x2 -> x1, Pallas kernels: 109 us -> 84.5 us  [body(): pl.pallas_call(functools.partial(kernel, nseg, ngrp), out_shape=(near, fa...]
    unnamed x9 -> x10, local copies, waits for them, and re-layouts: 5.69 us -> 7.07 us
where the time goes in v1:
time: 92.4 us; the launch traced here: 92.2 us
  Pallas kernels  84.5 us (91%)
  local copies, waits for them, and re-layouts  7.07 us (8%)
    pallas_call x1, Pallas kernels, body(): pl.pallas_call(functools.partial(kernel, nseg, ngrp), out_shape=(near, fa...  84.5 us
    unnamed x10, local copies, waits for them, and re-layouts  7.07 us

profile of v1, /device:TPU:0, one launch (start us, length us, event | category | flops | bytes accessed | tf_op | source)
XLA Modules:
  0.0 92.2 jit_solution(2018381232357844740)
XLA Ops:
  0.6 0.0 copy-start
  0.6 1.4 %copy-done = bf16[8,2,128,384]{3,2,1,0:T(8,128)(2,1)S(1)} copy-done((bf16[8,2,128,384]{3,2,1,0:T(8,128)(2,1)S(1)}, bf16[8,2,128,384]{3,2,1,0:T(8,128)(2,1)}, u32[]{:S(2)}) %copy-start) | copy-done | bytes 1572888
  2.0 0.0 copy-start.1
  2.0 0.8 copy-done.1
  2.8 0.0 copy-start.2
  2.8 0.7 copy-done.2
  3.5 0.0 copy-start.3
  3.5 0.7 copy-done.3
  4.2 84.5 %shard_map.59 = (bf16[2,2,384,1536]{3,2,1,0:T(8,128)(2,1)S(1)}, bf16[8,4,2,128,128]{4,3,2,1,0:T(8,128)(2,1)S(1)}) custom-call(s32[2,2]{1,0:T(2,128)S(1)} %copy-done.3, s32[8,3,4,8]{3,2,1,0:T(4,128)S(1)} %bitcast.6, s32[8,8]{1,0:T(8,128)S(1)} %bitcast.7, bf16[8,2,128,384]{3,2,1,0:T(8,128)(2,1)S(1)} %copy-done), custom_call_target="tpu_custom_call" | custom-call | tf_op jit(solution)/shard_map/pallas_call | solution.py:478
  88.7 2.2 %copy.8 = bf16[2,2,384,1536]{3,2,1,0:T(8,128)(2,1)} copy(bf16[2,2,384,1536]{3,2,1,0:T(8,128)(2,1)S(1)} %get-tuple-element.8) | data formatting | bytes 9437184
  90.9 1.3 %copy.9 = bf16[1,1,8,4,2,128,128]{6,5,4,3,2,1,0:T(8,128)(2,1)} copy(bf16[1,1,8,4,2,128,128]{6,5,4,3,2,1,0:T(8,128)(2,1)S(1)} %bitcast.5) | data formatting | bytes 4194304
Async XLA Ops:
  0.6 1.4 %copy-start = (bf16[8,2,128,384]{3,2,1,0:T(8,128)(2,1)S(1)}, bf16[8,2,128,384]{3,2,1,0:T(8,128)(2,1)}, u32[]{:S(2)}) copy-start(bf16[8,2,128,384]{3,2,1,0:T(8,128)(2,1)} %spectra.1) | copy-start | bytes 4718596
  2.0 0.8 copy-start.1
  2.8 0.7 copy-start.2
  3.5 0.7 copy-start.3

commit v2 on v1

--- a/solution.py
+++ b/solution.py
@@ -17,6 +17,7 @@
 DEPTH = W * 2 * BAND_MAX
 PIECES = 2 * BLK_DEV
 LEVELS = 4
+PARTS = 2
 CORES = 2
 
 
@@ -136,6 +137,10 @@
                     self.arrive(inside & there, far * low + other, q, ways, use)
 
 
+def part_rows(part):
+    return pl.ds(part * (DEPTH // PARTS), DEPTH // PARTS)
+
+
 class Line:
     def __init__(self, low, own, bufs, send, recv):
         self.low, self.own, self.bufs, self.send, self.recv = low, own, bufs, send, recv
@@ -149,13 +154,14 @@
     def buf(self, d, way):
         return self.bufs[self.slot(d, way)]
 
-    def move(self, way, d, q):
+    def move(self, way, d, q, part):
         at = self.slot(d + 1, way)
+        rows = part_rows(part)
         piece = pltpu.make_async_remote_copy(
-            src_ref=self.buf(d, way).at[q] if d else self.own.at[q],
-            dst_ref=self.bufs[at].at[q],
-            send_sem=self.send.at[way, d, q],
-            recv_sem=self.recv.at[at, q],
+            src_ref=(self.buf(d, way) if d else self.own).at[q, rows],
+            dst_ref=self.bufs[at].at[q, rows],
+            send_sem=self.send.at[way, d, q, part],
+            recv_sem=self.recv.at[at, q, part],
             device_id={"seg": self.me + (self.low if way else -self.low)},
             device_id_type=MESH,
         )
@@ -169,11 +175,13 @@
 
         @pl.when((z + 1 < LEVELS) & (z != LEVELS - 2))
         def _():
-            self.move(1, 0, q)
+            for part in range(PARTS):
+                self.move(1, 0, q, part)
 
         @pl.when((z > 0) & (z != 1))
         def _():
-            self.move(0, 0, q)
+            for part in range(PARTS):
+                self.move(0, 0, q, part)
 
     def there(self, d):
         z = self.z
@@ -182,28 +190,32 @@
             left, right = left & (z != LEVELS - 1), right & (z != 0)
         return ((left, z - d, z + 1 < LEVELS, 1), (right, z + d, z > 0, 0))
 
-    def arrive(self, d, q):
-        for here, _, on, way in self.there(d):
-
-            @pl.when(here)
-            def _():
-                if not self.closing:
-                    at = self.slot(d, way)
-                    piece = self.bufs[at].at[q]
-                    pltpu.make_async_copy(piece, piece, self.recv.at[at, q]).wait()
-
-                if d + 1 < LEVELS:
-
-                    @pl.when(on)
-                    def _():
-                        self.move(way, d, q)
+    def arrive(self, d, q, then=None):
+        for part in range(PARTS):
+            for here, _, on, way in self.there(d):
+
+                @pl.when(here)
+                def _():
+                    if not self.closing:
+                        at = self.slot(d, way)
+                        piece = self.bufs[at].at[q, part_rows(part)]
+                        pltpu.make_async_copy(piece, piece, self.recv.at[at, q, part]).wait()
+
+                    if d + 1 < LEVELS:
+
+                        @pl.when(on)
+                        def _():
+                            self.move(way, d, q, part)
+
+                    if then is not None:
+                        then(q, part)
 
 
 def kernel(
-    nseg, ngrp, bins, lists, counts, spectra, near, far,
-    spec, cols, left, right, two, three, side, grp_buf, ops, stage, end_stage,
+    nseg, ngrp, bins_in, lists_in, counts_in, spectra, near_out, far_out,
+    bins, lists, counts, near, far, spec, cols, left, right, two, three, side, grp_buf, ops, stage, end_stage,
     spec_sem, line_send, line_recv, side_send, side_recv, grp_send, grp_recv,
-    far_send, end_send, far_recv, move,
+    far_send, end_send, far_recv, pass_send, pass_recv, small_sem, out_sem, move, near_sem,
 ):
     low = nseg // LEVELS
     slots = far.shape[1]
@@ -212,6 +224,7 @@
     me, z = line.me, line.z
     y = lax.rem(me, low)
     mates = [lax.rem(y + e, low) for e in range(1, low)]
+    before = lax.rem(y + low - 1, low)
     is_end = (z == 0) | (z == LEVELS - 1)
     inner = (z == 1) | (z == LEVELS - 2)
     end = jnp.where(z == 1, 0, LEVELS - 1)
@@ -222,6 +235,12 @@
             spectra.at[:, :, :, m * BLOCK : (m + 1) * BLOCK], spec.at[m % 2], spec_sem.at[m % 2]
         )
 
+    small = [
+        pltpu.make_async_copy(a, b, small_sem.at[k])
+        for k, (a, b) in enumerate(((bins_in, bins), (lists_in, lists), (counts_in, counts)))
+    ]
+    for copy in small:
+        copy.start()
     load(0).start()
     load(1).start()
 
@@ -266,6 +285,8 @@
 
         lax.fori_loop(0, count, step, 0)
 
+    for copy in small:
+        copy.wait()
     for m in range(BLK_DEV):
         load(m).wait()
         whiten(m, bins, spec, cols)
@@ -320,14 +341,34 @@
         dst[c, 0] = prod[:BLOCK]
         dst[c, 1] = prod[BLOCK:]
 
-    def level_pairs(buf, src, c):
+    def pass_on(q, part):
+        rows = part_rows(part)
+        piece = pltpu.make_async_remote_copy(
+            src_ref=three.at[q, rows],
+            dst_ref=left.at[q, rows],
+            send_sem=pass_send.at[q, part],
+            recv_sem=pass_recv.at[q, part],
+            device_id={"seg": z * low + mates[0]},
+            device_id_type=MESH,
+        )
+        if line.closing:
+            piece.wait_send()
+        else:
+            piece.start()
+
+    def passed(q):
+        for part in range(PARTS):
+            piece = left.at[q, part_rows(part)]
+            pltpu.make_async_copy(piece, piece, pass_recv.at[q, part]).wait()
+
+    def level_pairs(buf, src, c, others):
         t = src * low + y
         pair(me, y, buf, t, far.at[t], c)
-        for mate in mates:
+        for mate in others:
             pair(z * low + mate, mate, buf, t, stage.at[mate, src], c)
 
-    def hand_over(src):
-        for mate in mates:
+    def hand_over(src, others):
+        for mate in others:
             piece = pltpu.make_async_remote_copy(
                 src_ref=stage.at[mate, src],
                 dst_ref=far.at[src * low + y],
@@ -392,37 +433,48 @@
 
                     @pl.when(here)
                     def _():
-                        level_pairs(line.buf(1, way), src, q)
+                        level_pairs(line.buf(1, way), src, q, mates)
 
                         @pl.when(q == slots - 1)
                         def _():
-                            hand_over(src)
+                            hand_over(src, mates)
 
     def later(d):
         def step(q):
             if d < LEVELS:
-                line.arrive(d, q)
+                line.arrive(d, q, pass_on if d == LEVELS - 1 else None)
             grp.step(d, q, None if grp.closing else use_near)
 
         loop(step)
 
     def after(d):
+        last = d == LEVELS - 1
+        others = mates[1:] if last else mates
         for here, src, _, way in line.there(d):
 
             @pl.when(here)
             def _():
                 if not line.closing:
-                    loop(lambda c: level_pairs(line.buf(d, way), src, c), slots)
-                hand_over(src)
+                    loop(lambda c: level_pairs(line.buf(d, way), src, c, others), slots)
+                hand_over(src, others)
+                if last and not line.closing:
+                    loop(passed)
+                    t = src * low + before
+                    loop(lambda c: pair(me, y, left, t, far.at[t], c), slots)
 
     loop(first)
     own.wait()
     far[me] = jnp.zeros(far.shape[1:], far.dtype)
     for_end()
     loop(second)
+    near_copy = pltpu.make_async_copy(near, near_out, near_sem)
+    if grp.high < 3:
+        near_copy.start()
     after(2)
     for d in range(3, max(LEVELS, grp.high + 1)):
         later(d)
+        if d == grp.high:
+            near_copy.start()
         if d < LEVELS:
             after(d)
 
@@ -442,26 +494,37 @@
         for other in [y] + mates:
             end_copy(other).wait_send()
 
+    def far_copy(t):
+        return pltpu.make_async_copy(far.at[t], far_out.at[t], out_sem.at[t])
+
     def landed(t):
         tz, ty = lax.div(t, low), lax.rem(t, low)
 
-        @pl.when(((ty != y) & (tz != z)) | (is_end & (tz == beside) & (ty == y)))
+        handed = (ty != y) & (tz != z) & ~(is_end & (tz == LEVELS - 1 - z) & (ty == before))
+
+        @pl.when(handed | (is_end & (tz == beside) & (ty == y)))
         def _():
             pltpu.make_async_copy(far.at[t], far.at[t], far_recv.at[t]).wait()
 
+        far_copy(t).start()
+
     loop(landed, nseg)
+    loop(lambda t: far_copy(t).wait(), nseg)
+    near_copy.wait()
 
 
 def body(nseg, ngrp, spectra, band_bins, far_list, far_count):
     slots = far_list.shape[3]
     low = nseg // LEVELS
-    smem = pl.BlockSpec(memory_space=pltpu.SMEM)
-    whole = pl.BlockSpec(memory_space=pltpu.VMEM)
+    hbm = pl.BlockSpec(memory_space=pl.ANY)
     sems = pltpu.SemaphoreType.DMA
     half = jnp.bfloat16
+    small = (band_bins, jnp.transpose(far_list[0], (0, 3, 2, 1)), far_count[0])
     near = jax.ShapeDtypeStruct((2, 2, BLK_DEV * BLOCK, ngrp * BLK_DEV * BLOCK), half)
     far = jax.ShapeDtypeStruct((nseg, slots, 2, BLOCK, BLOCK), half)
     buffers = [
+        pltpu.VMEM(near.shape, half),
+        pltpu.VMEM(far.shape, half),
         pltpu.VMEM((2, W, 2, F, BLOCK), half),
         pltpu.VMEM((PIECES, DEPTH, BLOCK), half),
         pltpu.VMEM((PIECES, DEPTH, BLOCK), half),
@@ -474,17 +537,19 @@
         pltpu.VMEM((low, LEVELS, slots, 2, BLOCK, BLOCK), half),
         pltpu.VMEM((low, slots, 2, BLOCK, BLOCK), half),
     ]
-    vmem = sum(math.prod(a.shape) * 2 for a in buffers + [near, far]) + 2 * 1024 * 1024
+    vmem = max(57, sum(math.prod(a.shape) * 2 for a in buffers) // 1024**2 + 3) * 1024**2
     near, far = pl.pallas_call(
         functools.partial(kernel, nseg, ngrp),
         out_shape=(near, far),
-        in_specs=[smem, smem, smem, pl.BlockSpec(memory_space=pl.ANY)],
-        out_specs=(whole, whole),
-        scratch_shapes=buffers
+        in_specs=[hbm] * 4,
+        out_specs=(hbm, hbm),
+        scratch_shapes=[pltpu.SMEM(a.shape, jnp.int32) for a in small]
+        + buffers
         + [
+
             sems((2,)),
-            sems((2, LEVELS, PIECES)),
-            sems((LEVELS, PIECES)),
+            sems((2, LEVELS, PIECES, PARTS)),
+            sems((LEVELS, PIECES, PARTS)),
             sems((low, PIECES)),
             sems((low, PIECES)),
             sems((4, ngrp, PIECES)),
@@ -492,12 +557,17 @@
             sems((low, LEVELS)),
             sems((low,)),
             sems((nseg,)),
+            sems((PIECES, PARTS)),
+            sems((PIECES, PARTS)),
+            sems((3,)),
+            sems((nseg,)),
+            sems,
             sems,
         ],
         compiler_params=pltpu.CompilerParams(
             collective_id=0, has_side_effects=True, vmem_limit_bytes=vmem
         ),
-    )(band_bins, jnp.transpose(far_list[0], (0, 3, 2, 1)), far_count[0], spectra)
+    )(*small, spectra)
     return (near, far[None, None])
 
 

time: 92.4 us -> 91 us (0.985)
    unnamed x10 -> x4, local copies, waits for them, and re-layouts: 7.07 us -> 6.3 us
where the time goes in v2:
time: 91 us; the launch traced here: 90.9 us
  Pallas kernels  83.9 us (92%)
  local copies, waits for them, and re-layouts  6.3 us (7%)
    pallas_call x1, Pallas kernels, body(): pl.pallas_call(functools.partial(kernel, nseg, ngrp), out_shape=(near, fa...  83.9 us
    unnamed x4, local copies, waits for them, and re-layouts  6.3 us

profile of v2, /device:TPU:0, one launch (start us, length us, event | category | flops | bytes accessed | tf_op | source)
XLA Modules:
  0.0 90.9 jit_solution(5928266855608332678)
XLA Ops:
  0.6 83.9 %shard_map.59 = (bf16[2,2,384,1536]{3,2,1,0:T(8,128)(2,1)}, bf16[8,4,2,128,128]{4,3,2,1,0:T(8,128)(2,1)}) custom-call(s32[2,2]{1,0:T(2,128)} %bins_in.1, s32[8,3,4,8]{3,2,1,0:T(4,128)} %bitcast.6, s32[8,8]{1,0:T(8,128)} %bitcast.7, bf16[8,2,128,384]{3,2,1,0:T(8,128)(2,1)} %spectra.1), custom_call_target="tpu_custom_call" | custom-call | tf_op jit(solution)/shard_map/pallas_call | solution.py:541
  84.6 0.0 copy-start
  84.6 5.0 %copy.8 = bf16[2,2,384,1536]{3,2,1,0:T(8,128)(2,1)} copy(bf16[2,2,384,1536]{3,2,1,0:T(8,128)(2,1)} %get-tuple-element.8) | data formatting | bytes 9437184
  89.5 0.0 copy-done
  89.5 1.3 %copy.9 = bf16[1,1,8,4,2,128,128]{6,5,4,3,2,1,0:T(8,128)(2,1)} copy(bf16[1,1,8,4,2,128,128]{6,5,4,3,2,1,0:T(8,128)(2,1)S(1)} %bitcast.5) | data formatting | bytes 4194304
Async XLA Ops:
  84.6 5.0 %copy-start = (bf16[8,4,2,128,128]{4,3,2,1,0:T(8,128)(2,1)S(1)}, bf16[8,4,2,128,128]{4,3,2,1,0:T(8,128)(2,1)}, u32[]{:S(2)}) copy-start(bf16[8,4,2,128,128]{4,3,2,1,0:T(8,128)(2,1)} %get-tuple-element.5) | copy-start | bytes 6291460

commit v3 on v2

--- a/solution.py
+++ b/solution.py
@@ -18,6 +18,7 @@
 PIECES = 2 * BLK_DEV
 LEVELS = 4
 PARTS = 2
+LIMIT = 62 * 1024**2
 CORES = 2
 
 
@@ -25,11 +26,11 @@
 MESH = pl.DeviceIdType.MESH
 
 
-def whiten(m, bins, spec, cols):
+def whiten(m, small, spec, cols):
     power = jnp.zeros((F, BLOCK), jnp.float32)
     for w in range(W):
         for p in range(2):
-            values = spec[m % 2, w, p].astype(jnp.float32)
+            values = spec[w, p, :, m * BLOCK : (m + 1) * BLOCK].astype(jnp.float32)
             power = power + values * values
     f = lax.broadcasted_iota(jnp.int32, (F, F), 0)
     g = lax.broadcasted_iota(jnp.int32, (F, F), 1)
@@ -37,12 +38,13 @@
     totals = jnp.sum(window, axis=1, keepdims=True) * W
     level = jnp.dot(window, power, precision=HIGH, preferred_element_type=jnp.float32) / totals
     gain = lax.rsqrt(level + 1e-06)
-    ahead = jnp.full((BAND_MAX, BLOCK), bins[0, 0], jnp.int32) == 0
+    here = slice(m * BLOCK, (m + 1) * BLOCK)
+    ahead = jnp.full((BAND_MAX, BLOCK), small[0, 4, 0, 0], jnp.int32) == 0
     for p in range(2):
         for w in range(W):
             at = slice((p * W + w) * BAND_MAX, (p * W + w + 1) * BAND_MAX)
-            low = spec[m % 2, w, p, :BAND_MAX].astype(jnp.float32) * gain[:BAND_MAX]
-            high = spec[m % 2, w, p, F - BAND_MAX :].astype(jnp.float32) * gain[F - BAND_MAX :]
+            low = spec[w, p, :BAND_MAX, here].astype(jnp.float32) * gain[:BAND_MAX]
+            high = spec[w, p, F - BAND_MAX :, here].astype(jnp.float32) * gain[F - BAND_MAX :]
             cols[m * 2, at] = jnp.where(ahead, low, high).astype(jnp.bfloat16)
             cols[m * 2 + 1, at] = jnp.where(ahead, high, low).astype(jnp.bfloat16)
 
@@ -146,6 +148,8 @@
         self.low, self.own, self.bufs, self.send, self.recv = low, own, bufs, send, recv
         self.me = lax.axis_index("seg")
         self.z = lax.div(self.me, low)
+        self.late = lax.rem(lax.axis_index("grp"), CORES) == CORES - 1
+        self.turns = low == 2 and CORES == 2
         self.closing = False
 
     def slot(self, d, way):
@@ -186,9 +190,25 @@
     def there(self, d):
         z = self.z
         left, right = z - d >= 0, z + d < LEVELS
+        on_right, on_left = z + 1 < LEVELS, z > 0
         if d == 1:
             left, right = left & (z != LEVELS - 1), right & (z != 0)
-        return ((left, z - d, z + 1 < LEVELS, 1), (right, z + d, z > 0, 0))
+        if self.turns and d == 1:
+            first = jnp.logical_not(self.late) & (not self.closing)
+            on_right, on_left = on_right & (first | (z != 1)), on_left & (first | (z != LEVELS - 2))
+        elif self.turns and d == 2:
+            on_right, on_left = on_right & self.late, on_left & self.late
+        elif self.turns:
+            left, right = left & self.late, right & self.late
+        return ((left, z - d, on_right, 1), (right, z + d, on_left, 0))
+
+    def cross(self, q):
+        for at, way in ((1, 1), (LEVELS - 2, 0)):
+
+            @pl.when(self.z == at)
+            def _():
+                for part in range(PARTS):
+                    self.move(way, 1, q, part)
 
     def arrive(self, d, q, then=None):
         for part in range(PARTS):
@@ -212,10 +232,10 @@
 
 
 def kernel(
-    nseg, ngrp, bins_in, lists_in, counts_in, spectra, near_out, far_out,
-    bins, lists, counts, near, far, spec, cols, left, right, two, three, side, grp_buf, ops, stage, end_stage,
-    spec_sem, line_send, line_recv, side_send, side_recv, grp_send, grp_recv,
-    far_send, end_send, far_recv, pass_send, pass_recv, small_sem, out_sem, move, near_sem,
+    nseg, ngrp, small, spec, near, far, cols, left, right, two, three, side, grp_buf, ops, stage, end_stage,
+    line_send, line_recv, side_send, side_recv, grp_send, grp_recv,
+    far_send, end_send, far_recv, pass_send, pass_recv,
+    turn_stage, turn_send, rows_send, rows_recv, go, move,
 ):
     low = nseg // LEVELS
     slots = far.shape[1]
@@ -230,20 +250,6 @@
     end = jnp.where(z == 1, 0, LEVELS - 1)
     beside = jnp.where(z == 0, 1, LEVELS - 2)
 
-    def load(m):
-        return pltpu.make_async_copy(
-            spectra.at[:, :, :, m * BLOCK : (m + 1) * BLOCK], spec.at[m % 2], spec_sem.at[m % 2]
-        )
-
-    small = [
-        pltpu.make_async_copy(a, b, small_sem.at[k])
-        for k, (a, b) in enumerate(((bins_in, bins), (lists_in, lists), (counts_in, counts)))
-    ]
-    for copy in small:
-        copy.start()
-    load(0).start()
-    load(1).start()
-
     barrier = pltpu.get_barrier_semaphore()
 
     def greet(seg):
@@ -257,6 +263,14 @@
 
     for mate in mates:
         greet(z * low + mate)
+        if line.turns:
+
+            @pl.when(is_end)
+            def _():
+                greet(beside * low + mate)
+
+    late = line.late
+    early = jnp.logical_not(late)
     grp.greet(barrier)
 
     def side_copy(e, q):
@@ -285,15 +299,12 @@
 
         lax.fori_loop(0, count, step, 0)
 
-    for copy in small:
-        copy.wait()
     for m in range(BLK_DEV):
-        load(m).wait()
-        whiten(m, bins, spec, cols)
-        if m + 2 < BLK_DEV:
-            load(m + 2).start()
+        whiten(m, small, spec, cols)
         if m == 0:
             inner_peers = jnp.where(z + 1 < LEVELS, 1, 0) + jnp.where(z > 0, 1, 0)
+            if line.turns:
+                inner_peers += jnp.where(inner, low - 1, 0)
             pl.semaphore_wait(barrier, inner_peers + (low - 1) + grp.peers())
         begin(2 * m)
         begin(2 * m + 1)
@@ -306,7 +317,7 @@
     def operands(slot, q, piece):
         band = lax.rem(q, 2)
         bin_of = lax.rem(lax.broadcasted_iota(jnp.int32, (1, DEPTH), 1), BAND_MAX)
-        live = jnp.where(bin_of < bins[band, 1], 1.0, 0.0).astype(jnp.float32)
+        live = jnp.where(bin_of < small[band, 4, 1, 0], 1.0, 0.0).astype(jnp.float32)
         rows = jnp.transpose(piece.astype(jnp.float32)) * live
         ops[slot, q, :BLOCK] = rows.astype(jnp.bfloat16)
         ops[slot, q, BLOCK:, :half] = rows[:, half:].astype(jnp.bfloat16)
@@ -315,7 +326,7 @@
     loop(lambda q: operands(y, q, cols[q]))
 
     def scale(band):
-        return lax.rsqrt(jnp.full((1, BLOCK), W * bins[band, 1], jnp.int32).astype(jnp.float32))
+        return lax.rsqrt(jnp.full((1, BLOCK), W * small[band, 4, 1, 0], jnp.int32).astype(jnp.float32))
 
     def near_from(piece, src, q):
         m, band = lax.div(q, 2), lax.rem(q, 2)
@@ -332,8 +343,8 @@
     loop(lambda q: near_from(cols[q], grp.me, q))
 
     def pair(owner, slot, src, t, dst, c):
-        i, m, band = lists[owner, 0, c, t], lists[owner, 1, c, t], lists[owner, 2, c, t]
-        factor = jnp.where(c < counts[owner, t], scale(band), 0.0)
+        i, m, band = small[owner, 0, c, t], small[owner, 1, c, t], small[owner, 2, c, t]
+        factor = jnp.where(c < small[owner, 3, 0, t], scale(band), 0.0)
         prod = jnp.dot(
             ops[slot, i * 2 + band], src[m * 2 + band], preferred_element_type=jnp.float32
         )
@@ -409,6 +420,35 @@
                 )
                 end_copy(other).start()
 
+    def rows_copy(q):
+        return pltpu.make_async_remote_copy(
+            src_ref=side.at[mates[0], q],
+            dst_ref=three.at[q],
+            send_sem=rows_send.at[q],
+            recv_sem=rows_recv.at[q],
+            device_id={"seg": beside * low + y},
+            device_id_type=MESH,
+        )
+
+    def turn_copy(k):
+        t = (LEVELS - 1 - end) * low + y
+        return pltpu.make_async_remote_copy(
+            src_ref=turn_stage.at[k],
+            dst_ref=far.at[t],
+            send_sem=turn_send.at[k],
+            recv_sem=far_recv.at[t],
+            device_id={"seg": end * low + (mates[0] if k else y)},
+            device_id_type=MESH,
+        )
+
+    def turn_pairs():
+        t = (LEVELS - 1 - end) * low + y
+        for k, owner in enumerate((y, mates[0])):
+            loop(
+                lambda c: pair(end * low + owner, low + k, two, t, turn_stage.at[k], c), slots
+            )
+            turn_copy(k).start()
+
     def first(q):
         line.arrive(1, q)
         grp.step(1, q, None if grp.closing else use_near)
@@ -418,10 +458,25 @@
                     side.at[mate, q], side.at[mate, q], side_recv.at[mate, q]
                 ).wait()
                 operands(mate, q, side[mate, q])
+        if line.turns:
+
+            @pl.when(is_end & early)
+            def _():
+                if line.closing:
+                    rows_copy(q).wait_send()
+                else:
+                    rows_copy(q).start()
 
     def second(q):
         line.arrive(2, q)
         grp.step(2, q, None if grp.closing else use_near)
+        if line.turns and not line.closing:
+
+            @pl.when(inner & early)
+            def _():
+                pltpu.make_async_copy(three.at[q], three.at[q], rows_recv.at[q]).wait()
+                operands(low + 1, q, three[q])
+
         if not line.closing:
 
             @pl.when(q < slots)
@@ -466,15 +521,29 @@
     own.wait()
     far[me] = jnp.zeros(far.shape[1:], far.dtype)
     for_end()
+    if line.turns:
+
+        @pl.when(inner & late)
+        def _():
+            pl.semaphore_wait(go, 1)
+            loop(line.cross)
+
     loop(second)
-    near_copy = pltpu.make_async_copy(near, near_out, near_sem)
-    if grp.high < 3:
-        near_copy.start()
+    if line.turns:
+
+        @pl.when(inner & early)
+        def _():
+            line.closing = True
+            loop(line.cross)
+            line.closing = False
+            pl.semaphore_signal(
+                go, inc=1, device_id={"grp": grp.me + 1}, device_id_type=MESH
+            )
+            turn_pairs()
+
     after(2)
     for d in range(3, max(LEVELS, grp.high + 1)):
         later(d)
-        if d == grp.high:
-            near_copy.start()
         if d < LEVELS:
             after(d)
 
@@ -494,38 +563,52 @@
         for other in [y] + mates:
             end_copy(other).wait_send()
 
-    def far_copy(t):
-        return pltpu.make_async_copy(far.at[t], far_out.at[t], out_sem.at[t])
+    if line.turns:
+
+        @pl.when(inner & late)
+        def _():
+            loop(line.cross)
+
+        @pl.when(inner & early)
+        def _():
+            for k in range(2):
+                turn_copy(k).wait_send()
 
     def landed(t):
         tz, ty = lax.div(t, low), lax.rem(t, low)
 
-        handed = (ty != y) & (tz != z) & ~(is_end & (tz == LEVELS - 1 - z) & (ty == before))
-
-        @pl.when(handed | (is_end & (tz == beside) & (ty == y)))
+        across = is_end & (tz == LEVELS - 1 - z)
+        passed_on = across & (ty == before)
+        handed = is_end & (tz == beside) & (ty == y)
+        if line.turns:
+            passed_on, handed = passed_on & late, handed | (across & (ty == y) & early)
+
+        @pl.when(handed | ((ty != y) & (tz != z) & jnp.logical_not(passed_on)))
         def _():
             pltpu.make_async_copy(far.at[t], far.at[t], far_recv.at[t]).wait()
 
-        far_copy(t).start()
-
     loop(landed, nseg)
-    loop(lambda t: far_copy(t).wait(), nseg)
-    near_copy.wait()
 
 
 def body(nseg, ngrp, spectra, band_bins, far_list, far_count):
     slots = far_list.shape[3]
     low = nseg // LEVELS
-    hbm = pl.BlockSpec(memory_space=pl.ANY)
+    smem = pl.BlockSpec(memory_space=pltpu.SMEM)
+    whole = pl.BlockSpec(memory_space=pltpu.VMEM)
     sems = pltpu.SemaphoreType.DMA
     half = jnp.bfloat16
-    small = (band_bins, jnp.transpose(far_list[0], (0, 3, 2, 1)), far_count[0])
+    shape = (nseg, 1, slots, nseg)
+    small = jnp.concatenate(
+        [
+            jnp.transpose(far_list[0], (0, 3, 2, 1)),
+            jnp.broadcast_to(far_count[0][:, None, None], shape),
+            jnp.pad(band_bins[:, None, :, None], [(0, n - k) for n, k in zip(shape, (2, 1, 2, 1))]),
+        ],
+        axis=1,
+    )
     near = jax.ShapeDtypeStruct((2, 2, BLK_DEV * BLOCK, ngrp * BLK_DEV * BLOCK), half)
     far = jax.ShapeDtypeStruct((nseg, slots, 2, BLOCK, BLOCK), half)
     buffers = [
-        pltpu.VMEM(near.shape, half),
-        pltpu.VMEM(far.shape, half),
-        pltpu.VMEM((2, W, 2, F, BLOCK), half),
         pltpu.VMEM((PIECES, DEPTH, BLOCK), half),
         pltpu.VMEM((PIECES, DEPTH, BLOCK), half),
         pltpu.VMEM((PIECES, DEPTH, BLOCK), half),
@@ -533,21 +616,20 @@
         pltpu.VMEM((PIECES, DEPTH, BLOCK), half),
         pltpu.VMEM((low, PIECES, DEPTH, BLOCK), half),
         pltpu.VMEM((ngrp, PIECES, DEPTH, BLOCK), half),
-        pltpu.VMEM((low + 1, PIECES, 2 * BLOCK, DEPTH), half),
+        pltpu.VMEM((low + (2 if low == 2 else 1), PIECES, 2 * BLOCK, DEPTH), half),
         pltpu.VMEM((low, LEVELS, slots, 2, BLOCK, BLOCK), half),
         pltpu.VMEM((low, slots, 2, BLOCK, BLOCK), half),
     ]
-    vmem = max(57, sum(math.prod(a.shape) * 2 for a in buffers) // 1024**2 + 3) * 1024**2
+    kept = sum(math.prod(a.shape) * 2 for a in buffers + [near, far, spectra])
+    vmem = min(kept + 2 * 1024**2, LIMIT)
     near, far = pl.pallas_call(
         functools.partial(kernel, nseg, ngrp),
         out_shape=(near, far),
-        in_specs=[hbm] * 4,
-        out_specs=(hbm, hbm),
-        scratch_shapes=[pltpu.SMEM(a.shape, jnp.int32) for a in small]
-        + buffers
+        in_specs=[smem, whole],
+        out_specs=(whole, whole),
+        scratch_shapes=buffers
         + [
 
-            sems((2,)),
             sems((2, LEVELS, PIECES, PARTS)),
             sems((LEVELS, PIECES, PARTS)),
             sems((low, PIECES)),
@@ -559,15 +641,17 @@
             sems((nseg,)),
             sems((PIECES, PARTS)),
             sems((PIECES, PARTS)),
-            sems((3,)),
-            sems((nseg,)),
-            sems,
+            pltpu.VMEM((2, slots, 2, BLOCK, BLOCK), half),
+            sems((2,)),
+            sems((PIECES,)),
+            sems((PIECES,)),
+            pltpu.SemaphoreType.REGULAR,
             sems,
         ],
         compiler_params=pltpu.CompilerParams(
             collective_id=0, has_side_effects=True, vmem_limit_bytes=vmem
         ),
-    )(*small, spectra)
+    )(small, spectra)
     return (near, far[None, None])
 
 

time: 91 us -> 84.1 us (0.924)
  the two profiles are of different devices: /device:TPU:0 before, /device:TPU:1 now
where the time goes in v3:
time: 84.1 us; the launch traced here: 83.8 us
  Pallas kernels  76 us (90%)
  local copies, waits for them, and re-layouts  6.37 us (8%)
    pallas_call x1, Pallas kernels, body(): pl.pallas_call(functools.partial(kernel, nseg, ngrp), out_shape=(near, fa...  76 us
    unnamed x4, local copies, waits for them, and re-layouts  4.91 us

profile of v3, /device:TPU:1, one launch (start us, length us, event | category | flops | bytes accessed | tf_op | source)
XLA Modules:
  0.0 83.8 jit_solution(3396315058465443666)
XLA Ops:
  0.6 0.8 copy.6
  1.4 0.7 broadcast_in_dim.14
  2.1 0.8 pad_add_fusion.small
  2.9 0.0 copy-start
  2.9 1.4 %copy-done = bf16[8,2,128,384]{3,2,1,0:T(8,128)(2,1)S(1)} copy-done((bf16[8,2,128,384]{3,2,1,0:T(8,128)(2,1)S(1)}, bf16[8,2,128,384]{3,2,1,0:T(8,128)(2,1)}, u32[]{:S(2)}) %copy-start) | copy-done | bytes 1572888
  4.3 76.0 %shard_map.59 = (bf16[2,2,384,1536]{3,2,1,0:T(8,128)(2,1)S(1)}, bf16[8,4,2,128,128]{4,3,2,1,0:T(8,128)(2,1)S(1)}) custom-call(s32[8,5,4,8]{3,2,1,0:T(4,128)S(1)} %pad_add_fusion.small, bf16[8,2,128,384]{3,2,1,0:T(8,128)(2,1)S(1)} %copy-done), custom_call_target="tpu_custom_call" | custom-call | tf_op jit(solution)/shard_map/pallas_call | solution.py:625
  80.3 2.2 %copy.9 = bf16[2,2,384,1536]{3,2,1,0:T(8,128)(2,1)} copy(bf16[2,2,384,1536]{3,2,1,0:T(8,128)(2,1)S(1)} %get-tuple-element.8) | data formatting | bytes 9437184
  82.5 1.3 %copy.10 = bf16[1,1,8,4,2,128,128]{6,5,4,3,2,1,0:T(8,128)(2,1)} copy(bf16[1,1,8,4,2,128,128]{6,5,4,3,2,1,0:T(8,128)(2,1)S(1)} %bitcast.6) | data formatting | bytes 4194304
Async XLA Ops:
  2.9 1.4 %copy-start = (bf16[8,2,128,384]{3,2,1,0:T(8,128)(2,1)S(1)}, bf16[8,2,128,384]{3,2,1,0:T(8,128)(2,1)}, u32[]{:S(2)}) copy-start(bf16[8,2,128,384]{3,2,1,0:T(8,128)(2,1)} %spec.1) | copy-start | bytes 4718596

commit v4 on v3

--- a/solution.py
+++ b/solution.py
@@ -39,7 +39,7 @@
     level = jnp.dot(window, power, precision=HIGH, preferred_element_type=jnp.float32) / totals
     gain = lax.rsqrt(level + 1e-06)
     here = slice(m * BLOCK, (m + 1) * BLOCK)
-    ahead = jnp.full((BAND_MAX, BLOCK), small[0, 4, 0, 0], jnp.int32) == 0
+    ahead = jnp.full((BAND_MAX, BLOCK), small[small.shape[0] - 1, 0, 0], jnp.int32) == 0
     for p in range(2):
         for w in range(W):
             at = slice((p * W + w) * BAND_MAX, (p * W + w + 1) * BAND_MAX)
@@ -317,7 +317,7 @@
     def operands(slot, q, piece):
         band = lax.rem(q, 2)
         bin_of = lax.rem(lax.broadcasted_iota(jnp.int32, (1, DEPTH), 1), BAND_MAX)
-        live = jnp.where(bin_of < small[band, 4, 1, 0], 1.0, 0.0).astype(jnp.float32)
+        live = jnp.where(bin_of < small[small.shape[0] - 1, band, 1], 1.0, 0.0).astype(jnp.float32)
         rows = jnp.transpose(piece.astype(jnp.float32)) * live
         ops[slot, q, :BLOCK] = rows.astype(jnp.bfloat16)
         ops[slot, q, BLOCK:, :half] = rows[:, half:].astype(jnp.bfloat16)
@@ -326,7 +326,7 @@
     loop(lambda q: operands(y, q, cols[q]))
 
     def scale(band):
-        return lax.rsqrt(jnp.full((1, BLOCK), W * small[band, 4, 1, 0], jnp.int32).astype(jnp.float32))
+        return lax.rsqrt(jnp.full((1, BLOCK), W * small[small.shape[0] - 1, band, 1], jnp.int32).astype(jnp.float32))
 
     def near_from(piece, src, q):
         m, band = lax.div(q, 2), lax.rem(q, 2)
@@ -343,8 +343,8 @@
     loop(lambda q: near_from(cols[q], grp.me, q))
 
     def pair(owner, slot, src, t, dst, c):
-        i, m, band = small[owner, 0, c, t], small[owner, 1, c, t], small[owner, 2, c, t]
-        factor = jnp.where(c < small[owner, 3, 0, t], scale(band), 0.0)
+        i, m, band = (small[owner * 3 + k, c, t] for k in range(3))
+        factor = jnp.where(c < small[nseg * 3 + lax.div(owner, slots), lax.rem(owner, slots), t], scale(band), 0.0)
         prod = jnp.dot(
             ops[slot, i * 2 + band], src[m * 2 + band], preferred_element_type=jnp.float32
         )
@@ -447,7 +447,11 @@
             loop(
                 lambda c: pair(end * low + owner, low + k, two, t, turn_stage.at[k], c), slots
             )
-            turn_copy(k).start()
+
+    def take_turn(step):
+        pl.semaphore_signal(
+            go, inc=1, device_id={"grp": grp.me + step}, device_id_type=MESH
+        )
 
     def first(q):
         line.arrive(1, q)
@@ -468,6 +472,15 @@
                     rows_copy(q).start()
 
     def second(q):
+        if line.turns and not line.closing:
+
+            @pl.when(inner & early & (q == PIECES - 1))
+            def _():
+                line.closing = True
+                loop(line.cross, PIECES - 1)
+                line.closing = False
+                take_turn(1)
+
         line.arrive(2, q)
         grp.step(2, q, None if grp.closing else use_near)
         if line.turns and not line.closing:
@@ -534,14 +547,23 @@
         @pl.when(inner & early)
         def _():
             line.closing = True
-            loop(line.cross)
+            line.cross(PIECES - 1)
             line.closing = False
-            pl.semaphore_signal(
-                go, inc=1, device_id={"grp": grp.me + 1}, device_id_type=MESH
-            )
             turn_pairs()
+            turn_copy(1).start()
+
+        @pl.when(inner & late)
+        def _():
+            take_turn(-1)
 
     after(2)
+    if line.turns:
+
+        @pl.when(inner & early)
+        def _():
+            pl.semaphore_wait(go, 1)
+            turn_copy(0).start()
+
     for d in range(3, max(LEVELS, grp.high + 1)):
         later(d)
         if d < LEVELS:
@@ -590,6 +612,21 @@
     loop(landed, nseg)
 
 
+def write_kernel(near, far, near_out, far_out, near_sem, far_sem):
+    copies = []
+    half = far.shape[0] // 2
+    for a in range(2):
+        for b in range(2):
+            copies.append((near.at[a, b], near_out.at[a, b], near_sem.at[a, b]))
+        at = pl.ds(a * half, half)
+        copies.append((far.at[at], far_out.at[at], far_sem.at[a]))
+    copies = [pltpu.make_async_copy(*copy) for copy in copies]
+    for copy in copies:
+        copy.start()
+    for copy in copies:
+        copy.wait()
+
+
 def body(nseg, ngrp, spectra, band_bins, far_list, far_count):
     slots = far_list.shape[3]
     low = nseg // LEVELS
@@ -597,15 +634,10 @@
     whole = pl.BlockSpec(memory_space=pltpu.VMEM)
     sems = pltpu.SemaphoreType.DMA
     half = jnp.bfloat16
-    shape = (nseg, 1, slots, nseg)
-    small = jnp.concatenate(
-        [
-            jnp.transpose(far_list[0], (0, 3, 2, 1)),
-            jnp.broadcast_to(far_count[0][:, None, None], shape),
-            jnp.pad(band_bins[:, None, :, None], [(0, n - k) for n, k in zip(shape, (2, 1, 2, 1))]),
-        ],
-        axis=1,
-    )
+    lists = jnp.transpose(far_list[0], (0, 3, 2, 1)).reshape(-1, slots, nseg)
+    counts = far_count.reshape(-1, slots, nseg)
+    bins = jnp.pad(band_bins[None], [(0, 0), (0, slots - 2), (0, nseg - 2)])
+    small = jnp.concatenate([lists, counts, bins])
     near = jax.ShapeDtypeStruct((2, 2, BLK_DEV * BLOCK, ngrp * BLK_DEV * BLOCK), half)
     far = jax.ShapeDtypeStruct((nseg, slots, 2, BLOCK, BLOCK), half)
     buffers = [
@@ -622,6 +654,7 @@
     ]
     kept = sum(math.prod(a.shape) * 2 for a in buffers + [near, far, spectra])
     vmem = min(kept + 2 * 1024**2, LIMIT)
+    near_shape, far_shape = near, far
     near, far = pl.pallas_call(
         functools.partial(kernel, nseg, ngrp),
         out_shape=(near, far),
@@ -652,6 +685,14 @@
             collective_id=0, has_side_effects=True, vmem_limit_bytes=vmem
         ),
     )(small, spectra)
+    near, far = pl.pallas_call(
+        write_kernel,
+        out_shape=(near_shape, far_shape),
+        in_specs=[pl.BlockSpec(memory_space=pl.ANY)] * 2,
+        out_specs=[pl.BlockSpec(memory_space=pl.ANY)] * 2,
+        scratch_shapes=[sems((2, 2)), sems((2,))],
+        compiler_params=pltpu.CompilerParams(vmem_limit_bytes=1024**2),
+    )(near, far)
     return (near, far[None, None])
 
 

time: 84.1 us -> 81.8 us (0.973)
  local copies, waits for them, and re-layouts: 6.37 us -> 1.4 us
  Pallas kernels: 76 us -> 78.7 us
    unnamed x4 -> x2, local copies, waits for them, and re-layouts: 4.91 us -> 1.4 us
    pallas_call x0 -> x1, Pallas kernels: none -> 2.89 us  [body(): pl.pallas_call(write_kernel, out_shape=(near_shape, far_shape), in_specs=...]
    broadcast_in_dim x2 -> x0, local copies, waits for them, and re-layouts: 1.46 us -> none  [the longest x1 0.77 us: body(): band_bins[:, None, :, None]]
where the time goes in v4:
time: 81.8 us; the launch traced here: 81.6 us
  Pallas kernels  78.7 us (96%)
  local copies, waits for them, and re-layouts  1.4 us (2%)
  other arithmetic  0.85 us (1%)
    pallas_call x1, Pallas kernels, body(): pl.pallas_call(functools.partial(kernel, nseg, ngrp), out_shape=(near, fa...  75.8 us
    pallas_call x1, Pallas kernels, body(): pl.pallas_call(write_kernel, out_shape=(near_shape, far_shape), in_specs=...  2.89 us

profile of v4, /device:TPU:1, one launch (start us, length us, event | category | flops | bytes accessed | tf_op | source)
XLA Modules:
  0.0 81.6 jit_solution(8286350095921840144)
XLA Ops:
  0.6 0.8 %pad_add_fusion.small = s32[27,4,8]{2,1,0:T(4,128)S(1)} fusion(s32[1,2,2]{2,1,0:T(2,128)} %bitcast.10, s32[2,4,8]{2,1,0:T(4,128)} %bitcast.9, s32[24,4,8]{2,1,0:T(4,128)} %bitcast.8), kind=kLoop, calls=%fused_computation | loop fusion | flops 1728 | bytes 6800 | tf_op jit(solution)/shard_map/concatenate | solution.py:640
  1.5 0.0 copy-start
  1.5 1.4 %copy-done = bf16[8,2,128,384]{3,2,1,0:T(8,128)(2,1)S(1)} copy-done((bf16[8,2,128,384]{3,2,1,0:T(8,128)(2,1)S(1)}, bf16[8,2,128,384]{3,2,1,0:T(8,128)(2,1)}, u32[]{:S(2)}) %copy-start) | copy-done | bytes 1572888
  2.9 75.8 %shard_map.59 = (bf16[2,2,384,1536]{3,2,1,0:T(8,128)(2,1)S(1)}, bf16[8,4,2,128,128]{4,3,2,1,0:T(8,128)(2,1)S(1)}) custom-call(s32[27,4,8]{2,1,0:T(4,128)S(1)} %pad_add_fusion.small, bf16[8,2,128,384]{3,2,1,0:T(8,128)(2,1)S(1)} %copy-done), custom_call_target="tpu_custom_call" | custom-call | tf_op jit(solution)/shard_map/pallas_call | solution.py:658
  78.7 2.9 %shard_map.60 = (bf16[2,2,384,1536]{3,2,1,0:T(8,128)(2,1)}, bf16[8,4,2,128,128]{4,3,2,1,0:T(8,128)(2,1)}) custom-call(bf16[2,2,384,1536]{3,2,1,0:T(8,128)(2,1)S(1)} %get-tuple-element.6.near, bf16[8,4,2,128,128]{4,3,2,1,0:T(8,128)(2,1)S(1)} %get-tuple-element.7.far), custom_call_target="tpu_custom_call" | custom-call | tf_op jit(solution)/shard_map/pallas_call | solution.py:688
Async XLA Ops:
  1.5 1.4 %copy-start = (bf16[8,2,128,384]{3,2,1,0:T(8,128)(2,1)S(1)}, bf16[8,2,128,384]{3,2,1,0:T(8,128)(2,1)}, u32[]{:S(2)}) copy-start(bf16[8,2,128,384]{3,2,1,0:T(8,128)(2,1)} %spec.1) | copy-start | bytes 4718596

commit v5 on v4

--- a/solution.py
+++ b/solution.py
@@ -372,11 +372,12 @@
             piece = left.at[q, part_rows(part)]
             pltpu.make_async_copy(piece, piece, pass_recv.at[q, part]).wait()
 
-    def level_pairs(buf, src, c, others):
+    def level_pairs(buf, src, c, others, own=True):
         t = src * low + y
-        pair(me, y, buf, t, far.at[t], c)
         for mate in others:
             pair(z * low + mate, mate, buf, t, stage.at[mate, src], c)
+        if own:
+            pair(me, y, buf, t, far.at[t], c)
 
     def hand_over(src, others):
         for mate in others:
@@ -474,10 +475,10 @@
     def second(q):
         if line.turns and not line.closing:
 
-            @pl.when(inner & early & (q == PIECES - 1))
+            @pl.when(inner & early & (q == PIECES - 3))
             def _():
                 line.closing = True
-                loop(line.cross, PIECES - 1)
+                loop(line.cross, PIECES - 3)
                 line.closing = False
                 take_turn(1)
 
@@ -523,8 +524,11 @@
             @pl.when(here)
             def _():
                 if not line.closing:
-                    loop(lambda c: level_pairs(line.buf(d, way), src, c, others), slots)
+                    if others:
+                        loop(lambda c: level_pairs(line.buf(d, way), src, c, others, False), slots)
                 hand_over(src, others)
+                if not line.closing:
+                    loop(lambda c: level_pairs(line.buf(d, way), src, c, ()), slots)
                 if last and not line.closing:
                     loop(passed)
                     t = src * low + before
@@ -547,10 +551,11 @@
         @pl.when(inner & early)
         def _():
             line.closing = True
+            line.cross(PIECES - 3)
+            line.cross(PIECES - 2)
             line.cross(PIECES - 1)
             line.closing = False
             turn_pairs()
-            turn_copy(1).start()
 
         @pl.when(inner & late)
         def _():
@@ -562,6 +567,7 @@
         @pl.when(inner & early)
         def _():
             pl.semaphore_wait(go, 1)
+            turn_copy(1).start()
             turn_copy(0).start()
 
     for d in range(3, max(LEVELS, grp.high + 1)):

time: 81.8 us -> 77.9 us (0.952)
  the two profiles are of different devices: /device:TPU:1 before, /device:TPU:0 now
where the time goes in v5:
time: 77.9 us; the launch traced here: 76.6 us
  Pallas kernels  73.7 us (95%)
  local copies, waits for them, and re-layouts  1.4 us (2%)
  other arithmetic  0.85 us (1%)
    pallas_call x1, Pallas kernels, body(): pl.pallas_call(functools.partial(kernel, nseg, ngrp), out_shape=(near, fa...  70.8 us
    pallas_call x1, Pallas kernels, body(): pl.pallas_call(write_kernel, out_shape=(near_shape, far_shape), in_specs=...  2.89 us

profile of v5, /device:TPU:0, one launch (start us, length us, event | category | flops | bytes accessed | tf_op | source)
XLA Modules:
  0.0 76.6 jit_solution(16697045099621404873)
XLA Ops:
  0.6 0.8 %pad_add_fusion.small = s32[27,4,8]{2,1,0:T(4,128)S(1)} fusion(s32[1,2,2]{2,1,0:T(2,128)} %bitcast.10, s32[2,4,8]{2,1,0:T(4,128)} %bitcast.9, s32[24,4,8]{2,1,0:T(4,128)} %bitcast.8), kind=kLoop, calls=%fused_computation | loop fusion | flops 1728 | bytes 6800 | tf_op jit(solution)/shard_map/concatenate | solution.py:646
  1.5 0.0 copy-start
  1.5 1.4 %copy-done = bf16[8,2,128,384]{3,2,1,0:T(8,128)(2,1)S(1)} copy-done((bf16[8,2,128,384]{3,2,1,0:T(8,128)(2,1)S(1)}, bf16[8,2,128,384]{3,2,1,0:T(8,128)(2,1)}, u32[]{:S(2)}) %copy-start) | copy-done | bytes 1572888
  2.9 70.8 %shard_map.59 = (bf16[2,2,384,1536]{3,2,1,0:T(8,128)(2,1)S(1)}, bf16[8,4,2,128,128]{4,3,2,1,0:T(8,128)(2,1)S(1)}) custom-call(s32[27,4,8]{2,1,0:T(4,128)S(1)} %pad_add_fusion.small, bf16[8,2,128,384]{3,2,1,0:T(8,128)(2,1)S(1)} %copy-done), custom_call_target="tpu_custom_call" | custom-call | tf_op jit(solution)/shard_map/pallas_call | solution.py:664
  73.7 2.9 %shard_map.60 = (bf16[2,2,384,1536]{3,2,1,0:T(8,128)(2,1)}, bf16[8,4,2,128,128]{4,3,2,1,0:T(8,128)(2,1)}) custom-call(bf16[2,2,384,1536]{3,2,1,0:T(8,128)(2,1)S(1)} %get-tuple-element.6.near, bf16[8,4,2,128,128]{4,3,2,1,0:T(8,128)(2,1)S(1)} %get-tuple-element.7.far), custom_call_target="tpu_custom_call" | custom-call | tf_op jit(solution)/shard_map/pallas_call | solution.py:694
Async XLA Ops:
  1.5 1.4 %copy-start = (bf16[8,2,128,384]{3,2,1,0:T(8,128)(2,1)S(1)}, bf16[8,2,128,384]{3,2,1,0:T(8,128)(2,1)}, u32[]{:S(2)}) copy-start(bf16[8,2,128,384]{3,2,1,0:T(8,128)(2,1)} %spec.1) | copy-start | bytes 4718596

commit v6 on v5

--- a/solution.py
+++ b/solution.py
@@ -483,6 +483,12 @@
                 take_turn(1)
 
         line.arrive(2, q)
+        if line.turns and not line.closing:
+
+            @pl.when(inner & late & (q == PIECES - 1))
+            def _():
+                take_turn(-1)
+
         grp.step(2, q, None if grp.closing else use_near)
         if line.turns and not line.closing:
 
@@ -534,6 +540,19 @@
                     t = src * low + before
                     loop(lambda c: pair(me, y, left, t, far.at[t], c), slots)
 
+    def landed(t, last):
+        tz, ty = lax.div(t, low), lax.rem(t, low)
+        across = is_end & (tz == LEVELS - 1 - z)
+        passed_on = across & (ty == before)
+        handed = is_end & (tz == beside) & (ty == y)
+        if line.turns:
+            passed_on, handed = passed_on & late, handed | (across & (ty == y) & early)
+        now = across if last else jnp.logical_not(across)
+
+        @pl.when(now & (handed | ((ty != y) & (tz != z) & jnp.logical_not(passed_on))))
+        def _():
+            pltpu.make_async_copy(far.at[t], far.at[t], far_recv.at[t]).wait()
+
     loop(first)
     own.wait()
     far[me] = jnp.zeros(far.shape[1:], far.dtype)
@@ -557,10 +576,6 @@
             line.closing = False
             turn_pairs()
 
-        @pl.when(inner & late)
-        def _():
-            take_turn(-1)
-
     after(2)
     if line.turns:
 
@@ -569,11 +584,6 @@
             pl.semaphore_wait(go, 1)
             turn_copy(1).start()
             turn_copy(0).start()
-
-    for d in range(3, max(LEVELS, grp.high + 1)):
-        later(d)
-        if d < LEVELS:
-            after(d)
 
     line.closing = grp.closing = True
     loop(begin)
@@ -581,11 +591,19 @@
     after(1)
     loop(second)
     after(2)
+    loop(lambda t: landed(t, False), nseg)
+    line.closing = grp.closing = False
     for d in range(3, max(LEVELS, grp.high + 1)):
         later(d)
         if d < LEVELS:
             after(d)
 
+    line.closing = grp.closing = True
+    for d in range(3, max(LEVELS, grp.high + 1)):
+        later(d)
+        if d < LEVELS:
+            after(d)
+
     @pl.when(inner)
     def _():
         for other in [y] + mates:
@@ -602,20 +620,7 @@
             for k in range(2):
                 turn_copy(k).wait_send()
 
-    def landed(t):
-        tz, ty = lax.div(t, low), lax.rem(t, low)
-
-        across = is_end & (tz == LEVELS - 1 - z)
-        passed_on = across & (ty == before)
-        handed = is_end & (tz == beside) & (ty == y)
-        if line.turns:
-            passed_on, handed = passed_on & late, handed | (across & (ty == y) & early)
-
-        @pl.when(handed | ((ty != y) & (tz != z) & jnp.logical_not(passed_on)))
-        def _():
-            pltpu.make_async_copy(far.at[t], far.at[t], far_recv.at[t]).wait()
-
-    loop(landed, nseg)
+    loop(lambda k: landed((LEVELS - 1 - z) * low + k, True), low)
 
 
 def write_kernel(near, far, near_out, far_out, near_sem, far_sem):

time: 77.9 us -> 77 us (0.988); the launches traced: 76.6 us -> 76.6 us
  no operation moved by 1% of the time
where the time goes in v6:
time: 77 us; the launch traced here: 76.6 us
  Pallas kernels  73.7 us (96%)
  local copies, waits for them, and re-layouts  1.4 us (2%)
  other arithmetic  0.85 us (1%)
    pallas_call x1, Pallas kernels, body(): pl.pallas_call(functools.partial(kernel, nseg, ngrp), out_shape=(near, fa...  70.8 us
    pallas_call x1, Pallas kernels, body(): pl.pallas_call(write_kernel, out_shape=(near_shape, far_shape), in_specs=...  2.89 us

profile of v6, /device:TPU:0, one launch (start us, length us, event | category | flops | bytes accessed | tf_op | source)
XLA Modules:
  0.0 76.6 jit_solution(2773074932146369448)
XLA Ops:
  0.6 0.8 %pad_add_fusion.small = s32[27,4,8]{2,1,0:T(4,128)S(1)} fusion(s32[1,2,2]{2,1,0:T(2,128)} %bitcast.10, s32[2,4,8]{2,1,0:T(4,128)} %bitcast.9, s32[24,4,8]{2,1,0:T(4,128)} %bitcast.8), kind=kLoop, calls=%fused_computation | loop fusion | flops 1728 | bytes 6800 | tf_op jit(solution)/shard_map/concatenate | solution.py:651
  1.5 0.0 copy-start
  1.5 1.4 %copy-done = bf16[8,2,128,384]{3,2,1,0:T(8,128)(2,1)S(1)} copy-done((bf16[8,2,128,384]{3,2,1,0:T(8,128)(2,1)S(1)}, bf16[8,2,128,384]{3,2,1,0:T(8,128)(2,1)}, u32[]{:S(2)}) %copy-start) | copy-done | bytes 1572888
  2.9 70.8 %shard_map.59 = (bf16[2,2,384,1536]{3,2,1,0:T(8,128)(2,1)S(1)}, bf16[8,4,2,128,128]{4,3,2,1,0:T(8,128)(2,1)S(1)}) custom-call(s32[27,4,8]{2,1,0:T(4,128)S(1)} %pad_add_fusion.small, bf16[8,2,128,384]{3,2,1,0:T(8,128)(2,1)S(1)} %copy-done), custom_call_target="tpu_custom_call" | custom-call | tf_op jit(solution)/shard_map/pallas_call | solution.py:669
  73.7 2.9 %shard_map.60 = (bf16[2,2,384,1536]{3,2,1,0:T(8,128)(2,1)}, bf16[8,4,2,128,128]{4,3,2,1,0:T(8,128)(2,1)}) custom-call(bf16[2,2,384,1536]{3,2,1,0:T(8,128)(2,1)S(1)} %get-tuple-element.6.near, bf16[8,4,2,128,128]{4,3,2,1,0:T(8,128)(2,1)S(1)} %get-tuple-element.7.far), custom_call_target="tpu_custom_call" | custom-call | tf_op jit(solution)/shard_map/pallas_call | solution.py:699
Async XLA Ops:
  1.5 1.4 %copy-start = (bf16[8,2,128,384]{3,2,1,0:T(8,128)(2,1)S(1)}, bf16[8,2,128,384]{3,2,1,0:T(8,128)(2,1)}, u32[]{:S(2)}) copy-start(bf16[8,2,128,384]{3,2,1,0:T(8,128)(2,1)} %spec.1) | copy-start | bytes 4718596

commit v7 on v6

--- a/solution.py
+++ b/solution.py
@@ -236,6 +236,7 @@
     line_send, line_recv, side_send, side_recv, grp_send, grp_recv,
     far_send, end_send, far_recv, pass_send, pass_recv,
     turn_stage, turn_send, rows_send, rows_recv, go, move,
+    turn_in, over_send, over_recv,
 ):
     low = nseg // LEVELS
     slots = far.shape[1]
@@ -323,6 +324,7 @@
         ops[slot, q, BLOCK:, :half] = rows[:, half:].astype(jnp.bfloat16)
         ops[slot, q, BLOCK:, half:] = (-rows[:, :half]).astype(jnp.bfloat16)
 
+    line.arrive(1, 0)
     loop(lambda q: operands(y, q, cols[q]))
 
     def scale(band):
@@ -339,8 +341,6 @@
 
     def use_near(src, q):
         near_from(grp_buf[src, q], src, q)
-
-    loop(lambda q: near_from(cols[q], grp.me, q))
 
     def pair(owner, slot, src, t, dst, c):
         i, m, band = (small[owner * 3 + k, c, t] for k in range(3))
@@ -432,22 +432,34 @@
         )
 
     def turn_copy(k):
-        t = (LEVELS - 1 - end) * low + y
+        t = (LEVELS - 1 - end) * low + (before if k else y)
         return pltpu.make_async_remote_copy(
-            src_ref=turn_stage.at[k],
+            src_ref=turn_in if k else turn_stage.at[0],
             dst_ref=far.at[t],
             send_sem=turn_send.at[k],
             recv_sem=far_recv.at[t],
-            device_id={"seg": end * low + (mates[0] if k else y)},
+            device_id={"seg": end * low + y},
+            device_id_type=MESH,
+        )
+
+    def turn_over():
+        return pltpu.make_async_remote_copy(
+            src_ref=turn_stage.at[1],
+            dst_ref=turn_in,
+            send_sem=over_send,
+            recv_sem=over_recv,
+            device_id={"seg": z * low + mates[0]},
             device_id_type=MESH,
         )
 
     def turn_pairs():
         t = (LEVELS - 1 - end) * low + y
-        for k, owner in enumerate((y, mates[0])):
+        for k, owner in ((1, mates[0]), (0, y)) if line.turns else ():
             loop(
                 lambda c: pair(end * low + owner, low + k, two, t, turn_stage.at[k], c), slots
             )
+            if k:
+                turn_over().start()
 
     def take_turn(step):
         pl.semaphore_signal(
@@ -455,7 +467,15 @@
         )
 
     def first(q):
-        line.arrive(1, q)
+        if line.closing:
+            line.arrive(1, q)
+        else:
+
+            @pl.when(q > 0)
+            def _():
+                line.arrive(1, q)
+
+            near_from(cols[q], grp.me, q)
         grp.step(1, q, None if grp.closing else use_near)
         if not line.closing:
             for mate in mates:
@@ -582,8 +602,9 @@
         @pl.when(inner & early)
         def _():
             pl.semaphore_wait(go, 1)
+            turn_copy(0).start()
+            pltpu.make_async_copy(turn_in, turn_in, over_recv).wait()
             turn_copy(1).start()
-            turn_copy(0).start()
 
     line.closing = grp.closing = True
     loop(begin)
@@ -617,6 +638,7 @@
 
         @pl.when(inner & early)
         def _():
+            turn_over().wait_send()
             for k in range(2):
                 turn_copy(k).wait_send()
 
@@ -691,6 +713,9 @@
             sems((PIECES,)),
             pltpu.SemaphoreType.REGULAR,
             sems,
+            pltpu.VMEM((slots, 2, BLOCK, BLOCK), half),
+            sems,
+            sems,
         ],
         compiler_params=pltpu.CompilerParams(
             collective_id=0, has_side_effects=True, vmem_limit_bytes=vmem

time: 77 us -> 76.7 us (level)
  no operation moved by 1% of the time
where the time goes in v7:
time: 76.7 us; the launch traced here: 76.5 us
  Pallas kernels  73.6 us (96%)
  local copies, waits for them, and re-layouts  1.4 us (2%)
  other arithmetic  0.85 us (1%)
    pallas_call x1, Pallas kernels, body(): pl.pallas_call(functools.partial(kernel, nseg, ngrp), out_shape=(near, fa...  70.8 us
    pallas_call x1, Pallas kernels, body(): pl.pallas_call(write_kernel, out_shape=(near_shape, far_shape), in_specs=...  2.89 us

profile of v7, /device:TPU:0, one launch (start us, length us, event | category | flops | bytes accessed | tf_op | source)
XLA Modules:
  0.0 76.5 jit_solution(1057930660310258705)
XLA Ops:
  0.6 0.8 %pad_add_fusion.small = s32[27,4,8]{2,1,0:T(4,128)S(1)} fusion(s32[1,2,2]{2,1,0:T(2,128)} %bitcast.10, s32[2,4,8]{2,1,0:T(4,128)} %bitcast.9, s32[24,4,8]{2,1,0:T(4,128)} %bitcast.8), kind=kLoop, calls=%fused_computation | loop fusion | flops 1728 | bytes 6800 | tf_op jit(solution)/shard_map/concatenate | solution.py:673
  1.5 0.0 copy-start
  1.5 1.4 %copy-done = bf16[8,2,128,384]{3,2,1,0:T(8,128)(2,1)S(1)} copy-done((bf16[8,2,128,384]{3,2,1,0:T(8,128)(2,1)S(1)}, bf16[8,2,128,384]{3,2,1,0:T(8,128)(2,1)}, u32[]{:S(2)}) %copy-start) | copy-done | bytes 1572888
  2.9 70.8 %shard_map.59 = (bf16[2,2,384,1536]{3,2,1,0:T(8,128)(2,1)S(1)}, bf16[8,4,2,128,128]{4,3,2,1,0:T(8,128)(2,1)S(1)}) custom-call(s32[27,4,8]{2,1,0:T(4,128)S(1)} %pad_add_fusion.small, bf16[8,2,128,384]{3,2,1,0:T(8,128)(2,1)S(1)} %copy-done), custom_call_target="tpu_custom_call" | custom-call | tf_op jit(solution)/shard_map/pallas_call | solution.py:691
  73.7 2.9 %shard_map.60 = (bf16[2,2,384,1536]{3,2,1,0:T(8,128)(2,1)}, bf16[8,4,2,128,128]{4,3,2,1,0:T(8,128)(2,1)}) custom-call(bf16[2,2,384,1536]{3,2,1,0:T(8,128)(2,1)S(1)} %get-tuple-element.6.near, bf16[8,4,2,128,128]{4,3,2,1,0:T(8,128)(2,1)S(1)} %get-tuple-element.7.far), custom_call_target="tpu_custom_call" | custom-call | tf_op jit(solution)/shard_map/pallas_call | solution.py:724
Async XLA Ops:
  1.5 1.4 %copy-start = (bf16[8,2,128,384]{3,2,1,0:T(8,128)(2,1)S(1)}, bf16[8,2,128,384]{3,2,1,0:T(8,128)(2,1)}, u32[]{:S(2)}) copy-start(bf16[8,2,128,384]{3,2,1,0:T(8,128)(2,1)} %spec.1) | copy-start | bytes 4718596
